TPU v7x, 256 devices: a whole 4x4x8 slice. The times are simulated.
256 devices in a mesh: feat: 64 (over y, z, core), rep: 4 (over x).
Axes of the slice: x: 4, y: 4, z: 8, core: 2. Of those that a mesh axis runs over, the one named last changes fastest.
Arguments:
- node_feats: bfloat16 [1024, 131072], P('feat', 'rep'), may hold values from -6 to 6
- neighbour_blocks: int32 [4, 32, 8], P('rep'), may hold values from 0 to 255
- edge_weights: bfloat16 [4, 32, 8, 128, 128], P('rep'), may hold values from 0 to 0.0625
- block_weights: bfloat16 [4, 32, 128, 128], P('rep'), may hold values from 0 to 0.015625
- owners: int32 [4, 32], P('rep'), may hold values from 0 to 63, as said below
- self_weight: bfloat16 [1024, 512], P('feat'), may hold values from -0.1875 to 0.1875
- neigh_weight: bfloat16 [1024, 512], P('feat'), may hold values from -0.1875 to 0.1875
- bias_one: float32 [512], replicated, may hold values from -3 to 3
- self_out: bfloat16 [512, 128], replicated, may hold values from -0.25 to 0.25
- neigh_out: bfloat16 [512, 128], replicated, may hold values from -0.25 to 0.25
- bias_two: float32 [128], replicated, may hold values from -3 to 3
- logit_grads: bfloat16 [4, 8192, 128], P('rep', 'feat'), may hold values from -6 to 6
Outputs:
- logits: bfloat16 [4, 8192, 128], P('rep', 'feat')
- grad_self_weight: float32 [1024, 512], P('feat')
- grad_neigh_weight: float32 [1024, 512], P('feat')
- grad_bias_one: float32 [512], replicated
- grad_self_out: float32 [512, 128], replicated
- grad_neigh_out: float32 [512, 128], replicated
- grad_bias_two: float32 [128], replicated
Inputs may be any that keep to these rules, and one draw needn't show every extreme that they name: Within one group the owners are distinct device indices of feat.
All inputs are finite; a program needn't handle non-finite values.
Results may differ from a plain program's by a relative error of at most 0.006.
Values may be sent and summed in bfloat16 or wider, within the bound.
No kernel may reach another device: no remote copies, remote signals or barrier semaphores. Data moves between devices by JAX's collectives and lax.ppermute only.
A program may use at most 128 MiB of HBM per device.

v0:
```python
import jax
import jax.numpy as jnp
from jax import lax
from jax.sharding import PartitionSpec as P


def silu_grad(value):
    sig = jax.nn.sigmoid(value)
    return sig * (1.0 + value * (1.0 - sig))


def contract_rows(left, right):
    return lax.dot_general(
        left, right, (((0,), (0,)), ((), ())), preferred_element_type=jnp.float32
    )


def on_device(
    node_feats,
    neighbour_blocks,
    edge_weights,
    block_weights,
    owners,
    self_weight,
    neigh_weight,
    bias_one,
    self_out,
    neigh_out,
    bias_two,
    logit_grads,
):
    devices = lax.axis_size("feat")
    slice_width = node_feats.shape[0]
    block_rows = block_weights.shape[-1]
    layer_blocks = owners.shape[1]
    spread = node_feats.reshape(slice_width, -1, block_rows)
    picked = spread[:, neighbour_blocks[0]]
    gathered_in = jnp.einsum(
        "cbkj,bkij->cbi", picked, edge_weights[0], preferred_element_type=jnp.float32
    ).astype(jnp.bfloat16)
    own_part = spread[:, :layer_blocks]
    stacked = jnp.concatenate([own_part, gathered_in], 0)
    places = owners[0][:, None] == jnp.arange(devices, dtype=jnp.int32)[None, :]
    slotted = jnp.einsum(
        "cbi,bs->csi", stacked, places.astype(jnp.bfloat16), preferred_element_type=jnp.float32
    ).astype(jnp.bfloat16)
    my_index = lax.axis_index("feat")
    my_blocks = jnp.take(places, my_index, axis=1)
    filled = jnp.any(my_blocks).astype(jnp.float32)
    tile_mine = jnp.einsum(
        "bij,b->ij",
        block_weights[0],
        my_blocks.astype(jnp.bfloat16),
        preferred_element_type=jnp.float32,
    ).astype(jnp.bfloat16)
    flat_slots = slotted.reshape(2 * slice_width, devices * block_rows)
    weights_one = jnp.concatenate([self_weight, neigh_weight], 0)
    window = flat_slots
    pre = (
        lax.psum_scatter(
            contract_rows(window, weights_one), "feat", scatter_dimension=0, tiled=True
        )
        + bias_one
    )
    hidden = jax.nn.silu(pre).astype(jnp.bfloat16)
    mixed = jnp.dot(tile_mine, hidden, preferred_element_type=jnp.float32).astype(jnp.bfloat16)
    result = jnp.dot(hidden, self_out, preferred_element_type=jnp.float32)
    result = result + jnp.dot(mixed, neigh_out, preferred_element_type=jnp.float32) + bias_two
    out_block = (result * filled).astype(jnp.bfloat16)[None]
    upstream = logit_grads[0] * filled.astype(jnp.bfloat16)
    grad_self_out = contract_rows(hidden, upstream)
    grad_neigh_out = contract_rows(mixed, upstream)
    grad_bias_two = jnp.sum(upstream.astype(jnp.float32), 0)
    d_mixed = jnp.dot(upstream, neigh_out.T, preferred_element_type=jnp.float32).astype(
        jnp.bfloat16
    )
    d_hidden = jnp.dot(upstream, self_out.T, preferred_element_type=jnp.float32) + contract_rows(
        tile_mine, d_mixed
    )
    d_pre = (d_hidden * silu_grad(pre)).astype(jnp.bfloat16)
    grad_bias_one = jnp.sum(d_pre.astype(jnp.float32), 0)
    window = flat_slots
    first_grads = jnp.dot(
        window,
        lax.all_gather(d_pre, "feat", axis=0, tiled=True),
        preferred_element_type=jnp.float32,
    )
    summed = lax.psum(first_grads, "rep")
    heads = lax.psum((grad_self_out, grad_neigh_out, grad_bias_two, grad_bias_one), ("feat", "rep"))
    return (
        out_block,
        summed[:slice_width],
        summed[slice_width:],
        heads[3],
        heads[0],
        heads[1],
        heads[2],
    )


def solution(mesh):
    placed = (
        P("feat", "rep"),
        P("rep", None, None),
        P("rep", None, None, None, None),
        P("rep", None, None, None),
        P("rep", None),
        P("feat", None),
        P("feat", None),
        P(),
        P(),
        P(),
        P(),
        P("rep", "feat", None),
    )
    return jax.shard_map(
        on_device,
        mesh=mesh,
        in_specs=placed,
        out_specs=(P("rep", "feat", None), P("feat", None), P("feat", None), P(), P(), P(), P()),
        check_vma=False,
    )
```

profile of v0, /device:TPU:1, one launch (start us, length us, event | category | flops | bytes accessed | tf_op | source)
XLA Modules:
  0.0 621.7 jit_solution(3932891474088027171)
XLA Ops:
  7.2 0.0 copy-start
  7.2 0.0 copy-start.8
  7.2 0.0 copy-start.5
  7.2 0.0 copy-start.6
  7.2 0.0 reduce-scatter.2.cloned.1.call-start
  7.3 2.5 copy_bitcast_fusion
  9.7 0.7 compare_select_fusion
  10.4 0.1 copy.20
  10.5 0.1 reshape.93
  10.6 2.1 gather_fusion
  12.7 0.0 copy-start.1
  12.7 5.8 fusion
  18.5 0.0 copy-done.1
  18.5 0.2 copy.29
  18.7 0.0 copy-done.8
  18.7 0.3 convolution_convert_fusion
  19.0 0.0 copy-done.5
  19.0 0.0 copy-done.6
  19.0 8.1 %fusion.12 = f32[8192,512]{1,0:T(8,128)} fusion(bf16[4,8,64,128]{3,2,1,0:T(8,128)(2,1)S(1)} %bitcast.71, bf16[16,512]{1,0:T(8,128)(2,1)S(1)} %copy-done.5, bf16[16,512]{1,0:T(8,128)(2,1)S(1)} %copy-done.6), kind=kOutput, calls=%fused_computation.19 | convolution fusion | flops 268500992 | bytes 17334272 | tf_op jit(solution)/shard_map/dot_general | solution.py:13
  27.1 0.0 reduce-scatter.2.cloned.1.call-update
  27.2 0.0 all-gather.2.cloned.1.call-start
  27.2 0.6 fusion.47
  28.5 0.0 copy-done.2
  28.6 0.0 copy-done.3
  28.6 0.2 fusion.29
  28.8 0.0 copy-done
  28.8 0.7 fusion.8
  29.4 187.4 %reduce-scatter.2.cloned.1.call-done = f32[128,512]{1,0:T(8,128)} async-done(((f32[8192,512]{1,0:T(8,128)}), f32[128,512]{1,0:T(8,128)}) %reduce-scatter.2.cloned.1.call-update) | async-done | bytes 262160 | tf_op jit(solution)/shard_map/reduce_scatter | solution.py:60
  216.9 0.0 copy-done.4
  216.9 2.0 convert_reduce_fusion
  218.8 0.0 all-gather.2.cloned.1.call-update
  218.9 0.0 all-reduce.5.cloned.1.call-start
  219.0 1.0 multiply_convert_fusion
  220.0 0.2 convolution_convert_fusion.2
  220.2 0.9 fusion.25
  221.1 0.9 fusion.23
  222.0 83.2 %all-gather.2.cloned.1.call-done = bf16[8192,512]{1,0:T(8,128)(2,1)} async-done(((bf16[128,512]{1,0:T(8,128)(2,1)}), bf16[8192,512]{1,0:T(8,128)(2,1)}) %all-gather.2.cloned.1.call-update) | async-done | bytes 8388624 | tf_op jit(solution)/shard_map/all_gather | solution.py:85
  305.2 5.4 fusion.10
  310.6 0.0 all-reduce.5.cloned.1.call-update
  310.6 0.0 all-reduce.7.cloned.1.call-start
  310.7 0.2 fusion.51
  310.8 0.3 all-reduce.7.cloned.1.call-update
  311.2 0.8 fusion.7
  312.0 75.8 %all-reduce = (f32[512]{0:T(512)}, f32[128]{0:T(128)}) all-reduce(f32[512]{0:T(512)S(1)} %get-tuple-element.24, f32[128]{0:T(128)S(1)} %convert_reduce_fusion.1), channel_id=1, replica_groups=mesh['feat'=64,'rep'=4] {'feat','rep'}, use_global_device_ids=true, to_apply=%region_4.5 | all-reduce | flops 640 | bytes 5120 | tf_op jit(solution)/shard_map/psum | solution.py:89
  387.8 1.4 fusion.48
  389.2 222.7 %all-reduce.7.cloned.1.call-done = (f32[512,128]{1,0:T(8,128)}, f32[512,128]{1,0:T(8,128)}) async-done(((f32[512,128]{1,0:T(8,128)}, f32[512,128]{1,0:T(8,128)}), (f32[512,128]{1,0:T(8,128)}, f32[512,128]{1,0:T(8,128)})) %all-reduce.7.cloned.1.call-update) | async-done | bytes 524304 | tf_op jit(solution)/shard_map/psum | solution.py:89
  611.9 1.7 copy.49
  613.5 1.7 copy.50
  (13 shorter events, 0.1 us)
Async XLA Ops:
  7.2 21.6 %copy-start = (bf16[1,32,128,128]{3,2,1,0:T(8,128)(2,1)S(1)}, bf16[1,32,128,128]{3,2,1,0:T(8,128)(2,1)}, u32[]{:S(2)}) copy-start(bf16[1,32,128,128]{3,2,1,0:T(8,128)(2,1)} %param.15) | copy-start | bytes 3145732
  7.2 11.5 %copy-start.8 = (s32[1,32]{1,0:T(1,128)S(1)}, s32[1,32]{1,0:T(1,128)}, u32[]{:S(2)}) copy-start(s32[1,32]{1,0:T(1,128)} %param.16) | copy-start | bytes 388
  7.2 11.8 %copy-start.5 = (bf16[16,512]{1,0:T(8,128)(2,1)S(1)}, bf16[16,512]{1,0:T(8,128)(2,1)}, u32[]{:S(2)}) copy-start(bf16[16,512]{1,0:T(8,128)(2,1)} %param.18) | copy-start | bytes 49156
  7.2 11.8 %copy-start.6 = (bf16[16,512]{1,0:T(8,128)(2,1)S(1)}, bf16[16,512]{1,0:T(8,128)(2,1)}, u32[]{:S(2)}) copy-start(bf16[16,512]{1,0:T(8,128)(2,1)} %param.17) | copy-start | bytes 49156
  7.2 209.7 %reduce-scatter.2.cloned.1.call-start = ((), (), s32[]{:S(2)}) async-start(), calls=%async_computation.1 | async-start | bytes 17039360 | tf_op jit(solution)/shard_map/reduce_scatter | solution.py:60
  12.7 5.8 copy-start.1
  27.1 1.4 copy-start.2
  27.1 1.4 copy-start.3
  27.1 189.7 %copy-start.4 = (bf16[512,128]{1,0:T(8,128)(2,1)S(1)}, bf16[512,128]{1,0:T(8,128)(2,1)}, u32[]{:S(2)}) copy-start(bf16[512,128]{1,0:T(8,128)(2,1)} %param.21) | copy-start | bytes 393220
  27.1 189.7 %copy-start.7 = (f32[512]{0:T(512)S(1)}, f32[512]{0:T(512)}, u32[]{:S(2)}) copy-start(f32[512]{0:T(512)} %param.19) | copy-start | bytes 6148
  27.2 278.0 %all-gather.2.cloned.1.call-start = ((), (), s32[]{:S(2)}) async-start(), calls=%async_computation.2 | async-start | bytes 8519680 | tf_op jit(solution)/shard_map/all_gather | solution.py:85
  218.9 168.9 %all-reduce.5.cloned.1.call-start = ((), (), s32[]{:S(2)}) async-start(), calls=%async_computation.3 | async-start | bytes 131072 | tf_op jit(solution)/shard_map/psum | solution.py:88
  222.0 89.2 %copy-start.9 = (f32[128]{0:T(128)S(1)}, f32[128]{0:T(128)}, u32[]{:S(2)}) copy-start(f32[128]{0:T(128)} %param.22) | copy-start | bytes 1540
  310.6 301.3 %all-reduce.7.cloned.1.call-start = ((), (), s32[]{:S(2)}) async-start(), calls=%async_computation.4 | async-start | bytes 1048576 | tf_op jit(solution)/shard_map/psum | solution.py:89
Sparse Core Ops, SparseCore 0:
  27.3 189.5 reduce-scatter.1
  219.7 85.5 all-gather.1
  310.7 40.7 all-reduce.4
  358.5 253.3 all-reduce.6
where the time goes:
time: 623 us; the launch traced here: 622 us
  waiting for transfers between devices  494 us (79%)
  blocking collectives  75.8 us (12%)
  matrix products  25.3 us (4%)
  between operations  14.6 us (2%)
  local copies, waits for them, and re-layouts  9.72 us (2%)
    psum x1, waiting for transfers between devices, on_device(): lax.psum((grad_self_out, grad_neigh_out, grad_bias_two, grad_bias_one), (...  223 us
    reduce_scatter x1, waiting for transfers between devices, on_device(): lax.psum_scatter(contract_rows(window, weights_one), 'feat', scatter_dime...  187 us
    all_gather x1, waiting for transfers between devices, on_device(): lax.all_gather(d_pre, 'feat', axis=0, tiled=True)  83.2 us
    psum x1, blocking collectives, on_device(): lax.psum((grad_self_out, grad_neigh_out, grad_bias_two, grad_bias_one), (...  75.8 us
  transfers between devices with their start and end apart: 4, of which 3 were waited for; matrix products, arithmetic and copies ran while one was open for 1% of the time, Pallas kernels for 0%

commit v1 on v0

v1 whole, which is shorter than its diff:
```python
import jax
import jax.numpy as jnp
from jax import lax
from jax.sharding import Mesh, PartitionSpec as P

Y, Z, CORES, REPS = 4, 8, 2, 4
CHIPS = Y * Z
SWAP = [(0, 1), (1, 0)]


def silu_grad(value):
    sig = jax.nn.sigmoid(value)
    return sig * (1.0 + value * (1.0 - sig))


def contract_rows(left, right):
    return lax.dot_general(
        left, right, (((0,), (0,)), ((), ())), preferred_element_type=jnp.float32
    )


def exchange(value, axes):
    return lax.all_to_all(value, axes, 0, 0, tiled=True)


def to_all(value, axes, count):
    return exchange(jnp.broadcast_to(value[None], (count,) + value.shape), axes)


def on_device(
    node_feats,
    neighbour_blocks,
    edge_weights,
    block_weights,
    owners,
    self_weight,
    neigh_weight,
    bias_one,
    self_out,
    neigh_out,
    bias_two,
    logit_grads,
):
    width = node_feats.shape[0]
    rows = block_weights.shape[-1]
    layer_blocks = owners.shape[1]
    hid, out = self_out.shape
    chips = ("y", "z")
    core = lax.axis_index("core")
    first = core == 0
    me = lax.axis_index(("y", "z", "core"))

    spread = node_feats.reshape(width, -1, rows)
    picked = spread[:, neighbour_blocks[0]]
    gathered_in = jnp.einsum(
        "cbkj,bkij->cbi", picked, edge_weights[0], preferred_element_type=jnp.float32
    ).astype(jnp.bfloat16)
    stacked = jnp.concatenate([spread[:, :layer_blocks], gathered_in], 0)
    slots = jnp.arange(Y * Z * CORES, dtype=jnp.int32).reshape(Y, Z, CORES)
    slots = slots.transpose(1, 2, 0).reshape(1, -1)
    places = (owners[0][:, None] == slots).astype(jnp.bfloat16)
    slotted = jnp.einsum(
        "cbi,bs->csi", stacked, places, preferred_element_type=jnp.float32
    ).astype(jnp.bfloat16)
    half = Y * rows
    sent = slotted.reshape(2 * width, Z, CORES * half).transpose(1, 0, 2)
    weights_one = jnp.concatenate([self_weight, neigh_weight], 0)
    weights_one = jnp.broadcast_to(weights_one[None], (Z, 2 * width, hid))
    arrived = exchange(jnp.concatenate([sent, weights_one], 2), "z")
    arrived = arrived.reshape(Z * 2 * width, CORES * half + hid)
    weights_all = arrived[:, CORES * half :]
    feats_mine = lax.dynamic_slice_in_dim(arrived, core * half, half, 1)
    feats_other = lax.dynamic_slice_in_dim(arrived, (1 - core) * half, half, 1)

    my_blocks = owners[0] == me
    filled = jnp.any(my_blocks).astype(jnp.float32)
    tile_mine = jnp.einsum(
        "bij,b->ij",
        block_weights[0],
        my_blocks.astype(jnp.bfloat16),
        preferred_element_type=jnp.float32,
    ).astype(jnp.bfloat16)
    upstream = logit_grads[0] * filled.astype(jnp.bfloat16)

    given = lax.ppermute(contract_rows(feats_other, weights_all), "core", SWAP)
    partial = (contract_rows(feats_mine, weights_all) + given).astype(jnp.bfloat16)
    partial = exchange(partial.reshape(Y, rows, hid), "y")
    pre = jnp.sum(partial.astype(jnp.float32), 0) + bias_one

    hidden = jax.nn.silu(pre).astype(jnp.bfloat16)
    mixed = jnp.dot(tile_mine, hidden, preferred_element_type=jnp.float32).astype(jnp.bfloat16)
    result = jnp.dot(hidden, self_out, preferred_element_type=jnp.float32)
    result = result + jnp.dot(mixed, neigh_out, preferred_element_type=jnp.float32) + bias_two
    out_block = (result * filled).astype(jnp.bfloat16)[None]
    d_mixed = jnp.dot(upstream, neigh_out.T, preferred_element_type=jnp.float32).astype(
        jnp.bfloat16
    )
    d_hidden = jnp.dot(upstream, self_out.T, preferred_element_type=jnp.float32) + contract_rows(
        tile_mine, d_mixed
    )
    d_pre = (d_hidden * silu_grad(pre)).astype(jnp.bfloat16)

    heads = (contract_rows(hidden, upstream), contract_rows(mixed, upstream))
    bias = jnp.concatenate(
        [jnp.sum(d_pre.astype(jnp.float32), 0), jnp.sum(upstream.astype(jnp.float32), 0)]
    ).reshape(-1, out)
    kept = jnp.concatenate([jnp.where(first, heads[0], heads[1]), bias], 0)
    given = jnp.concatenate([jnp.where(first, heads[1], heads[0]), bias], 0)
    kept = (kept + lax.ppermute(given, "core", SWAP)).astype(jnp.bfloat16)

    pad = 16
    sums = jnp.concatenate(
        [
            jnp.broadcast_to(d_pre[None], (Y, rows, hid)),
            kept[:hid].reshape(Y, hid // Y, out),
        ],
        2,
    )
    bias = jnp.pad(kept[hid:].reshape(1, -1), ((0, pad - 1), (0, 0)))
    sums = jnp.concatenate([sums, jnp.broadcast_to(bias[None], (Y, pad, hid + out))], 1)
    sums = exchange(sums, "y")
    d_mine = sums[:, :rows, :hid].reshape(half, hid)
    kept = jnp.sum(sums[:, :rows, hid:].astype(jnp.float32), 0).astype(jnp.bfloat16)
    bias = jnp.sum(sums[:, rows].astype(jnp.float32), 0).astype(jnp.bfloat16)

    d_other = lax.ppermute(d_mine, "core", SWAP)
    grads = jnp.dot(feats_mine, d_mine, preferred_element_type=jnp.float32)
    grads = grads + jnp.dot(feats_other, d_other, preferred_element_type=jnp.float32)
    grads = grads.astype(jnp.bfloat16).reshape(Z, 2 * width, hid)
    share = hid // CHIPS
    bias = bias.reshape(-1, out)
    spare = 2 * width - share
    bias = jnp.pad(bias, ((0, spare - bias.shape[0]), (0, 0)))
    extra = jnp.concatenate(
        [kept.reshape(Z, share, out), jnp.broadcast_to(bias[None], (Z, spare, out))], 1
    )
    sums = exchange(jnp.concatenate([grads, extra], 2), "z")
    sums = jnp.sum(sums.astype(jnp.float32), 0)
    sums = jnp.sum(to_all(sums, "rep", REPS), 0)
    grads = sums[:, :hid]
    bias = sums[share:, hid:].reshape(-1)

    kept = to_all(sums[:share, hid:], chips, CHIPS).reshape(hid, out)
    given = lax.ppermute(kept, "core", SWAP)
    return (
        out_block,
        grads[:width],
        grads[width:],
        bias[:hid],
        jnp.where(first, kept, given),
        jnp.where(first, given, kept),
        bias[hid : hid + out],
    )


def solution(mesh):
    fine = Mesh(mesh.devices.reshape(Y, Z, CORES, REPS), ("y", "z", "core", "rep"))
    feat = ("y", "z", "core")
    placed = (
        P(feat, "rep"),
        P("rep", None, None),
        P("rep", None, None, None, None),
        P("rep", None, None, None),
        P("rep", None),
        P(feat, None),
        P(feat, None),
        P(),
        P(),
        P(),
        P(),
        P("rep", feat, None),
    )
    return jax.shard_map(
        on_device,
        mesh=fine,
        in_specs=placed,
        out_specs=(P("rep", feat, None), P(feat, None), P(feat, None), P(), P(), P(), P()),
        check_vma=False,
    )
```

time: 623 us -> 131 us (0.21)
  waiting for transfers between devices: 494 us -> 43.1 us
  blocking collectives: 75.8 us -> 40.2 us
  starting transfers between devices: 0.16 us -> 24.7 us
  matrix products: 25.3 us -> 12.1 us
  between operations: 14.6 us -> 1.7 us
    psum x2 -> x0, waiting for transfers between devices: 223 us -> none  [the longest x1 223 us: on_device(): lax.psum((grad_self_out, grad_neigh_out, grad_bias_two, grad_bias_one), (...]
    reduce_scatter x1 -> x0, waiting for transfers between devices: 187 us -> none  [on_device(): lax.psum_scatter(contract_rows(window, weights_one), 'feat', scatter_dime...]
    all_gather x1 -> x0, waiting for transfers between devices: 83.2 us -> none  [on_device(): lax.all_gather(d_pre, 'feat', axis=0, tiled=True)]
    psum x1 -> x0, blocking collectives: 75.8 us -> none  [on_device(): lax.psum((grad_self_out, grad_neigh_out, grad_bias_two, grad_bias_one), (...]
    all_to_all x0 -> x3, blocking collectives: none -> 40.2 us  [exchange(): return lax.all_to_all(value, axes, 0, 0, tiled=True)]
    all_to_all x0 -> x3, waiting for transfers between devices: none -> 39.6 us  [exchange(): return lax.all_to_all(value, axes, 0, 0, tiled=True)]
    all_to_all x0 -> x3, starting transfers between devices: none -> 17.2 us  [exchange(): return lax.all_to_all(value, axes, 0, 0, tiled=True)]
    dot_general x4 -> x5, matrix products: 11.9 us -> 3.48 us  [contract_rows(): lax.dot_general(left, right, (((0,), (0,)), ((), ())), preferred_element_...]
  transfers between devices with their start and end apart: 4 -> 7, of which waited for: 3 -> 6; matrix products, arithmetic and copies ran while one was open for 1% -> 4% of each run, Pallas kernels for 0% -> 0%
where the time goes in v1:
time: 131 us
  waiting for transfers between devices  43.1 us (33%)
  blocking collectives  40.2 us (31%)
  starting transfers between devices  24.7 us (19%)
  matrix products  12.1 us (9%)
  local copies, waits for them, and re-layouts  5.75 us (4%)
  other arithmetic  2.98 us (2%)
  between operations  1.7 us (1%)
    all_to_all x3, blocking collectives, exchange(): return lax.all_to_all(value, axes, 0, 0, tiled=True)  40.2 us
    all_to_all x3, waiting for transfers between devices, exchange(): return lax.all_to_all(value, axes, 0, 0, tiled=True)  39.6 us
    all_to_all x3, starting transfers between devices, exchange(): return lax.all_to_all(value, axes, 0, 0, tiled=True)  17.2 us
    dot_general x1, matrix products, on_device(): jnp.einsum('cbkj,bkij->cbi', picked, edge_weights[0], preferred_element_t...  5.67 us
    ppermute x1, starting transfers between devices, on_device(): given = lax.ppermute(kept, 'core', SWAP)  3.68 us
    dot_general x5, matrix products, contract_rows(): lax.dot_general(left, right, (((0,), (0,)), ((), ())), preferred_element_...  3.48 us
  transfers between devices with their start and end apart: 7, of which 6 were waited for; matrix products, arithmetic and copies ran while one was open for 4% of the time, Pallas kernels for 0%

profile of v1, /device:TPU:1, one launch (start us, length us, event | category | flops | bytes accessed | tf_op | source)
XLA Modules:
  0.0 130.6 jit_solution(18024770578790890380)
XLA Ops:
  0.7 1.5 %copy_bitcast_fusion = bf16[16,256,128]{2,0,1:T(8,128)(2,1)S(1)} fusion(bf16[16,32768]{1,0:T(8,128)(2,1)} %param.12), kind=kLoop, calls=%fused_computation.22 | loop fusion | bytes 2097152 | tf_op jit(solution)/shard_map/reshape | solution.py:53
  2.2 0.1 copy.28
  2.3 0.1 reshape.158
  2.4 0.8 gather_fusion
  3.2 0.1 reshape.143
  3.3 5.7 %fusion.13 = bf16[16,32,128]{2,0,1:T(8,128)(2,1)S(1)} fusion(bf16[16,32,8,128]{3,0,2,1:T(8,128)(2,1)S(1)} %bitcast.104, bf16[1,32,8,128,128]{4,3,2,1,0:T(8,128)(2,1)} %param.14), kind=kOutput, calls=%fused_computation.16 | convolution fusion | flops 134283264 | bytes 9568256 | tf_op jit(solution)/shard_map/cbkj,bkij->cbi/dot_general | solution.py:55
  9.1 0.4 fusion.3
  9.5 0.2 reshape.145
  9.7 0.3 copy.46
  10.1 0.9 pad_maximum_fusion
  11.0 9.0 %all-to-all-start = ((bf16[8,32,1536]{2,1,0:T(8,128)(2,1)}), bf16[8,32,1536]{2,1,0:T(8,128)(2,1)S(1)}, u32[]{:S(2)}, u32[]{:S(2)}) async-start(bf16[8,32,1536]{2,1,0:T(8,128)(2,1)} %pad_maximum_fusion), calls=%async_computation | async-start | bytes 1572864 | tf_op jit(solution)/shard_map/all_to_all | solution.py:23
  20.1 23.6 %all-to-all-done = bf16[8,32,1536]{2,1,0:T(8,128)(2,1)S(1)} async-done(((bf16[8,32,1536]{2,1,0:T(8,128)(2,1)}), bf16[8,32,1536]{2,1,0:T(8,128)(2,1)S(1)}, u32[]{:S(2)}, u32[]{:S(2)}) %all-to-all-start) | async-done | bytes 786464 | tf_op jit(solution)/shard_map/all_to_all | solution.py:23
  43.6 0.3 fusion.25
  44.0 0.6 collective-permute-start
  44.6 0.6 compare_reduce_fusion
  45.9 1.1 collective-permute-done
  47.0 2.4 %fusion.2 = bf16[512,512]{1,0:T(8,128)(2,1)} fusion(f32[512,512]{1,0:T(8,128)} %collective-permute-done, bf16[256,1536]{1,0:T(8,128)(2,1)S(1)} %bitcast.101, s32[]{:T(128)S(6)} %select_n.37), kind=kOutput, calls=%fused_computation.4 | convolution fusion | flops 134742016 | bytes 2097156 | tf_op jit(solution)/shard_map/dot_general | solution.py:17
  49.4 4.3 %all-to-all-start.1 = ((bf16[4,128,512]{2,1,0:T(8,128)(2,1)}), bf16[4,128,512]{2,1,0:T(8,128)(2,1)S(1)}, u32[]{:S(2)}, u32[]{:S(2)}) async-start(bf16[4,128,512]{2,1,0:T(8,128)(2,1)} %bitcast.12), calls=%async_computation.1 | async-start | bytes 1048576 | tf_op jit(solution)/shard_map/all_to_all | solution.py:23
  53.7 0.2 fusion.42
  53.9 0.7 fusion.20
  54.6 8.0 %all-to-all-done.1 = bf16[4,128,512]{2,1,0:T(8,128)(2,1)S(1)} async-done(((bf16[4,128,512]{2,1,0:T(8,128)(2,1)}), bf16[4,128,512]{2,1,0:T(8,128)(2,1)S(1)}, u32[]{:S(2)}, u32[]{:S(2)}) %all-to-all-start.1) | async-done | bytes 524320 | tf_op jit(solution)/shard_map/all_to_all | solution.py:23
  62.6 0.1 convert_reduce_fusion
  62.7 0.1 multiply_convert_fusion
  62.8 0.2 convolution_convert_fusion.2
  62.9 0.2 fusion.36
  63.2 0.4 convert_reduce_fusion.2
  63.5 0.2 broadcast_select_fusion.3
  63.8 1.6 %collective-permute-start.1 = (f32[517,128]{1,0:T(8,128)S(1)}, f32[517,128]{1,0:T(8,128)S(1)}, u32[]{:S(2)}, u32[]{:S(2)}) collective-permute-start(f32[517,128]{1,0:T(8,128)S(1)} %pad_maximum_fusion.2), channel_id=1, source_target_pairs={{0,4},{4,0},{1,5},{5,1},{2,6},{6,2},{3,7},{7,3},{8,12},{12,8},{9,1... | collective-permute-start | bytes 794120 | tf_op jit(solution)/shard_map/ppermute | solution.py:109
  65.4 1.1 collective-permute-done.1
  66.7 0.1 pad_maximum_fusion.1
  66.8 13.6 %all_to_all.30 = bf16[4,144,640]{2,1,0:T(8,128)(2,1)S(1)} all-to-all(bf16[4,144,640]{2,1,0:T(8,128)(2,1)S(1)} %pad_maximum_fusion.1), channel_id=1, replica_groups=mesh['y'=4,'z'=8,'core'=2,'rep'=4] {'y'}, dimensions={0} | all-to-all | bytes 1474560 | tf_op jit(solution)/shard_map/all_to_all | solution.py:23
  80.4 1.6 %collective-permute-start.2 = (bf16[512,512]{1,0:T(8,128)(2,1)S(1)}, bf16[512,512]{1,0:T(8,128)(2,1)S(1)}, u32[]{:S(2)}, u32[]{:S(2)}) collective-permute-start(bf16[512,512]{1,0:T(8,128)(2,1)S(1)} %bitcast.105), channel_id=1, source_target_pairs={{0,4},{4,0},{1,5},{5,1},{2,6},{6,2},{3,7},{7,3},{8,12},{12,8},{9,1... | collective-permute-start | bytes 1572872 | tf_op jit(solution)/shard_map/ppermute | solution.py:126
  82.1 0.3 fusion.30
  82.4 1.2 collective-permute-done.2
  83.5 0.3 fusion.4
  83.8 0.1 maximum_maximum_fusion
  83.9 16.1 %all_to_all.31 = bf16[8,32,640]{2,1,0:T(8,128)(2,1)S(1)} all-to-all(bf16[8,32,640]{2,1,0:T(8,128)(2,1)S(1)} %maximum_maximum_fusion), channel_id=1, replica_groups=mesh['y'=4,'z'=8,'core'=2,'rep'=4] {'z'}, dimensions={0} | all-to-all | bytes 655360 | tf_op jit(solution)/shard_map/all_to_all | solution.py:23
  100.1 10.5 %all_to_all.32 = f32[4,32,640]{2,1,0:T(8,128)S(1)} all-to-all(f32[4,32,640]{2,1,0:T(8,128)S(1)} %broadcast_in_dim.19), channel_id=1, replica_groups=mesh['y'=4,'z'=8,'core'=2,'rep'=4] {'rep'}, dimensions={0} | all-to-all | bytes 655360 | tf_op jit(solution)/shard_map/all_to_all | solution.py:23
  110.6 0.7 broadcast_in_dim.20
  111.4 3.9 %all-to-all-start.5 = ((f32[32,16,128]{2,1,0:T(8,128)}), f32[32,16,128]{2,1,0:T(8,128)S(1)}, u32[]{:S(2)}, u32[]{:S(2)}) async-start(f32[32,16,128]{2,1,0:T(8,128)} %broadcast_in_dim.20), calls=%async_computation.5 | async-start | bytes 524288 | tf_op jit(solution)/shard_map/all_to_all | solution.py:23
  115.2 0.2 fusion.70
  115.4 0.8 fusion.19
  116.2 0.6 slice_bitcast_fusion
  116.8 8.1 %all-to-all-done.5 = f32[32,16,128]{2,1,0:T(8,128)S(1)} async-done(((f32[32,16,128]{2,1,0:T(8,128)}), f32[32,16,128]{2,1,0:T(8,128)S(1)}, u32[]{:S(2)}, u32[]{:S(2)}) %all-to-all-start.5) | async-done | bytes 262176 | tf_op jit(solution)/shard_map/all_to_all | solution.py:23
  124.9 3.7 %collective-permute-start.3 = (f32[512,128]{1,0:T(8,128)S(1)}, f32[512,128]{1,0:T(8,128)S(1)}, u32[]{:S(2)}, u32[]{:S(2)}) collective-permute-start(f32[512,128]{1,0:T(8,128)S(1)} %bitcast.108), channel_id=1, source_target_pairs={{0,4},{4,0},{1,5},{5,1},{2,6},{6,2},{3,7},{7,3},{8,12},{12,8},{9,1... | collective-permute-start | bytes 786440 | tf_op jit(solution)/shard_map/ppermute | solution.py:144
  128.6 0.5 slice_bitcast_fusion.2
  129.1 0.6 fusion.67
  129.7 0.9 broadcast_select_fusion
  (46 shorter events, 0.5 us)
Async XLA Ops:
  0.6 53.3 %copy-start = (bf16[1,32,128,128]{3,2,1,0:T(8,128)(2,1)S(1)}, bf16[1,32,128,128]{3,2,1,0:T(8,128)(2,1)}, u32[]{:S(2)}) copy-start(bf16[1,32,128,128]{3,2,1,0:T(8,128)(2,1)} %param.15) | copy-start | bytes 3145732
  0.6 1.5 %copy-start.6 = (s32[1,32,8]{1,2,0:T(8,128)S(1)}, s32[1,32,8]{1,2,0:T(8,128)}, u32[]{:S(2)}) copy-start(s32[1,32,8]{1,2,0:T(8,128)} %param.13) | copy-start | bytes 3076
  3.3 5.7 %copy-start.7 = (s32[1,32]{1,0:T(1,128)S(1)}, s32[1,32]{1,0:T(1,128)}, u32[]{:S(2)}) copy-start(s32[1,32]{1,0:T(1,128)} %param.16) | copy-start | bytes 388
  9.1 1.0 copy-start.4
  9.1 1.0 copy-start.5
  11.0 32.6 %all-to-all-start = ((bf16[8,32,1536]{2,1,0:T(8,128)(2,1)}), bf16[8,32,1536]{2,1,0:T(8,128)(2,1)S(1)}, u32[]{:S(2)}, u32[]{:S(2)}) async-start(bf16[8,32,1536]{2,1,0:T(8,128)(2,1)} %pad_maximum_fusion), calls=%async_computation | async-start | bytes 1572864 | tf_op jit(solution)/shard_map/all_to_all | solution.py:23
  44.0 9.7 %copy-start.1 = (bf16[512,128]{1,0:T(8,128)(2,1)S(1)}, bf16[512,128]{1,0:T(8,128)(2,1)}, u32[]{:S(2)}) copy-start(bf16[512,128]{1,0:T(8,128)(2,1)} %param.20) | copy-start | bytes 393220
  44.0 9.7 %copy-start.2 = (bf16[1,128,128]{2,1,0:T(8,128)(2,1)S(1)}, bf16[1,128,128]{2,1,0:T(8,128)(2,1)}, u32[]{:S(2)}) copy-start(bf16[1,128,128]{2,1,0:T(8,128)(2,1)} %param.23) | copy-start | bytes 98308
  44.0 3.0 %collective-permute-start = (f32[512,512]{1,0:T(8,128)S(1)}, f32[512,512]{1,0:T(8,128)}, u32[]{:S(2)}, u32[]{:S(2)}) collective-permute-start(f32[512,512]{1,0:T(8,128)S(1)} %fusion.25), channel_id=1, source_target_pairs={{0,4},{4,0},{1,5},{5,1},{2,6},{6,2},{3,7},{7,3},{8,12},{12,8},{9,1... | collective-permute-start | bytes 3145736 | tf_op jit(solution)/shard_map/ppermute | solution.py:85
  49.4 13.3 %copy-start.8 = (f32[512]{0:T(512)S(1)}, f32[512]{0:T(512)}, u32[]{:S(2)}) copy-start(f32[512]{0:T(512)} %param.19) | copy-start | bytes 6148
  49.4 13.2 %all-to-all-start.1 = ((bf16[4,128,512]{2,1,0:T(8,128)(2,1)}), bf16[4,128,512]{2,1,0:T(8,128)(2,1)S(1)}, u32[]{:S(2)}, u32[]{:S(2)}) async-start(bf16[4,128,512]{2,1,0:T(8,128)(2,1)} %bitcast.12), calls=%async_computation.1 | async-start | bytes 1048576 | tf_op jit(solution)/shard_map/all_to_all | solution.py:23
  53.9 9.3 %copy-start.3 = (bf16[512,128]{1,0:T(8,128)(2,1)S(1)}, bf16[512,128]{1,0:T(8,128)(2,1)}, u32[]{:S(2)}) copy-start(bf16[512,128]{1,0:T(8,128)(2,1)} %param.21) | copy-start | bytes 393220
  63.8 2.8 %collective-permute-start.1 = (f32[517,128]{1,0:T(8,128)S(1)}, f32[517,128]{1,0:T(8,128)S(1)}, u32[]{:S(2)}, u32[]{:S(2)}) collective-permute-start(f32[517,128]{1,0:T(8,128)S(1)} %pad_maximum_fusion.2), channel_id=1, source_target_pairs={{0,4},{4,0},{1,5},{5,1},{2,6},{6,2},{3,7},{7,3},{8,12},{12,8},{9,1... | collective-permute-start | bytes 794120 | tf_op jit(solution)/shard_map/ppermute | solution.py:109
  80.4 3.1 %collective-permute-start.2 = (bf16[512,512]{1,0:T(8,128)(2,1)S(1)}, bf16[512,512]{1,0:T(8,128)(2,1)S(1)}, u32[]{:S(2)}, u32[]{:S(2)}) collective-permute-start(bf16[512,512]{1,0:T(8,128)(2,1)S(1)} %bitcast.105), channel_id=1, source_target_pairs={{0,4},{4,0},{1,5},{5,1},{2,6},{6,2},{3,7},{7,3},{8,12},{12,8},{9,1... | collective-permute-start | bytes 1572872 | tf_op jit(solution)/shard_map/ppermute | solution.py:126
  100.0 15.4 %copy-start.9 = (f32[128]{0:T(128)S(1)}, f32[128]{0:T(128)}, u32[]{:S(2)}) copy-start(f32[128]{0:T(128)} %param.22) | copy-start | bytes 1540
  111.4 13.5 %all-to-all-start.5 = ((f32[32,16,128]{2,1,0:T(8,128)}), f32[32,16,128]{2,1,0:T(8,128)S(1)}, u32[]{:S(2)}, u32[]{:S(2)}) async-start(f32[32,16,128]{2,1,0:T(8,128)} %broadcast_in_dim.20), calls=%async_computation.5 | async-start | bytes 524288 | tf_op jit(solution)/shard_map/all_to_all | solution.py:23
  124.9 4.8 %collective-permute-start.3 = (f32[512,128]{1,0:T(8,128)S(1)}, f32[512,128]{1,0:T(8,128)S(1)}, u32[]{:S(2)}, u32[]{:S(2)}) collective-permute-start(f32[512,128]{1,0:T(8,128)S(1)} %bitcast.108), channel_id=1, source_target_pairs={{0,4},{4,0},{1,5},{5,1},{2,6},{6,2},{3,7},{7,3},{8,12},{12,8},{9,1... | collective-permute-start | bytes 786440 | tf_op jit(solution)/shard_map/ppermute | solution.py:144

commit v2 on v1

v2 whole, which is shorter than its diff:
```python
import functools

import jax
import jax.numpy as jnp
from jax import lax
from jax.experimental import pallas as pl
from jax.experimental.pallas import tpu as pltpu
from jax.sharding import Mesh, PartitionSpec as P

Y, Z, CORES, REPS = 4, 8, 2, 4
CHIPS = Y * Z
SWAP = [(0, 1), (1, 0)]


def silu_grad(value):
    sig = jax.nn.sigmoid(value)
    return sig * (1.0 + value * (1.0 - sig))


def dot(left, right, left_dim, right_dim):
    return lax.dot_general(
        left, right, (((left_dim,), (right_dim,)), ((), ())), preferred_element_type=jnp.float32
    )


def exchange(value, axes):
    return lax.all_to_all(value, axes, 0, 0, tiled=True)


def to_all(value, axes, count):
    return exchange(jnp.broadcast_to(value[None], (count,) + value.shape), axes)


def swap(value):
    return lax.ppermute(value, "core", SWAP)


def shift(value, axis, count, by):
    return lax.ppermute(value, axis, [(i, (i + by) % count) for i in range(count)])


def paired(terms):
    return (terms[0] + terms[2]) + (terms[1] + terms[3])


def rep_sum(value):
    terms = [value] + [shift(value, "rep", REPS, by) for by in range(1, REPS)]
    return paired(terms)


def gather_kernel(neighbours, owners, place, feats, edges, own, near, out, *, per_step):
    step = pl.program_id(0)
    width = feats.shape[0]
    fan, rows = edges.shape[1], edges.shape[-1]
    layer_rows = Y * CORES * rows
    half = own.shape[1] // CORES

    @pl.when(step == 0)
    def _():
        out[:, :, half : half + layer_rows] = jnp.zeros((Z, 2 * width, layer_rows), out.dtype)
        for c in range(CORES):

            @pl.when(place[1] == c)
            def _(c=c):
                kept, given = c * half, (1 - c) * half
                for z in range(Z):
                    out[z, :width, :half] = own[:, kept : kept + half]
                    out[z, width:, :half] = near[:, kept : kept + half]
                    out[z, :width, half + layer_rows :] = own[:, given : given + half]
                    out[z, width:, half + layer_rows :] = near[:, given : given + half]

    for i in range(per_step):
        block = step * per_step + i
        starts = [pl.multiple_of(neighbours[block * fan + k] * rows, rows) for k in range(fan)]
        total = lax.dot_general(
            jnp.concatenate([feats[:, pl.ds(start, rows)] for start in starts], 1),
            jnp.concatenate([edges[i, k] for k in range(fan)], 1),
            (((1,), (1,)), ((), ())),
            preferred_element_type=jnp.float32,
        )
        owner = owners[block]
        core = owner & (CORES - 1)
        z = lax.shift_right_logical(owner, 1) & (Z - 1)
        y = (lax.shift_right_logical(owner, 4) - place[0]) & (Y - 1)
        lane = pl.multiple_of(half + (y * CORES + core) * rows, rows)
        out[z, :width, pl.ds(lane, rows)] = feats[:, pl.ds(pl.multiple_of(block * rows, rows), rows)]
        out[z, width:, pl.ds(lane, rows)] = total.astype(out.dtype)


def gather_rows(neighbours, owners, place, feats, edges, own, near):
    blocks, fan, rows, _ = edges.shape
    width = feats.shape[0]
    columns = Y * CORES * rows + own.shape[1]
    per_step = 8
    return pl.pallas_call(
        functools.partial(gather_kernel, per_step=per_step),
        out_shape=jax.ShapeDtypeStruct((Z, 2 * width, columns), feats.dtype),
        grid_spec=pltpu.PrefetchScalarGridSpec(
            num_scalar_prefetch=3,
            grid=(blocks // per_step,),
            in_specs=[
                pl.BlockSpec(feats.shape, lambda i, *_: (0, 0)),
                pl.BlockSpec((per_step, fan, rows, rows), lambda i, *_: (i, 0, 0, 0)),
                pl.BlockSpec(own.shape, lambda i, *_: (0, 0)),
                pl.BlockSpec(near.shape, lambda i, *_: (0, 0)),
            ],
            out_specs=pl.BlockSpec((Z, 2 * width, columns), lambda i, *_: (0, 0, 0)),
        ),
        compiler_params=pltpu.CompilerParams(vmem_limit_bytes=56 * 1024 * 1024),
        cost_estimate=pl.CostEstimate(
            flops=2 * width * blocks * fan * rows * rows,
            bytes_accessed=2 * (edges.size + feats.size),
            transcendentals=0,
        ),
        name="gather_rows",
    )(neighbours.reshape(-1), owners, place, feats, edges, own, near)


def on_device(
    node_feats,
    neighbour_blocks,
    edge_weights,
    block_weights,
    owners,
    self_weight,
    neigh_weight,
    bias_one,
    self_out,
    neigh_out,
    bias_two,
    logit_grads,
):
    width = node_feats.shape[0]
    rows = block_weights.shape[-1]
    hid, out = self_out.shape
    half = hid // 2
    chips = ("y", "z")
    core = lax.axis_index("core")
    at_y = lax.axis_index("y")
    at_z = lax.axis_index("z")
    first = core == 0

    def columns(value, which):
        return lax.dynamic_slice_in_dim(value, which * half, half, value.ndim - 1)

    span = CORES * rows
    sent = gather_rows(
        neighbour_blocks[0],
        owners[0],
        jnp.stack([at_y, core]).astype(jnp.int32),
        node_feats,
        edge_weights[0],
        self_weight,
        neigh_weight,
    )
    arrived = exchange(sent, "z").reshape(Z * 2 * width, Y * span + hid)
    from_other = swap(arrived[:, half:])
    weights_mine, feats_mine = arrived[:, :half], arrived[:, half : half + Y * span]
    weights_other, feats_other = from_other[:, Y * span :], from_other[:, : Y * span]

    my_slots = (at_y * Z + at_z) * CORES + jnp.arange(CORES, dtype=jnp.int32)
    my_blocks = owners[0][None] == my_slots[:, None]
    filled = jnp.any(my_blocks, 1)
    tiles = jnp.einsum(
        "bij,cb->cij",
        block_weights[0],
        my_blocks.astype(jnp.bfloat16),
        preferred_element_type=jnp.float32,
    ).astype(jnp.bfloat16)
    up_mine = logit_grads[0]
    up_other = swap(up_mine)
    upstream = jnp.stack(
        [jnp.where(first, up_mine, up_other), jnp.where(first, up_other, up_mine)]
    )
    upstream = upstream * filled.astype(jnp.bfloat16)[:, None, None]
    up_rows = upstream.reshape(span, out)
    self_half = lax.dynamic_slice_in_dim(self_out, core * half, half, 0)
    neigh_half = lax.dynamic_slice_in_dim(neigh_out, core * half, half, 0)
    d_mixed = dot(up_rows, neigh_half, 1, 1).astype(jnp.bfloat16).reshape(CORES, rows, half)
    d_hidden = dot(up_rows, self_half, 1, 1) + jnp.concatenate(
        [dot(tiles[i], d_mixed[i], 0, 0) for i in range(CORES)], 0
    )

    partial = dot(feats_mine, weights_mine, 0, 0) + dot(feats_other, weights_other, 0, 0)
    partial = partial.astype(jnp.bfloat16).reshape(Y, span, half)
    pre = partial[0].astype(jnp.float32)
    for by in range(1, Y):
        pre = pre + shift(partial[by], "y", Y, by).astype(jnp.float32)
    pre = pre + columns(bias_one, core)

    hidden = jax.nn.silu(pre).astype(jnp.bfloat16)
    d_pre = (d_hidden * silu_grad(pre)).astype(jnp.bfloat16)
    mixed = jnp.concatenate(
        [dot(tiles[i], hidden[i * rows : (i + 1) * rows], 1, 0) for i in range(CORES)], 0
    ).astype(jnp.bfloat16)
    result = dot(hidden, self_half, 1, 0) + dot(mixed, neigh_half, 1, 0)
    result_mine = jnp.where(first, result[:rows], result[rows:])
    result_other = jnp.where(first, result[rows:], result[:rows])
    result = result_mine + swap(result_other) + bias_two
    mine_filled = jnp.where(first, filled[0], filled[1]).astype(jnp.float32)
    out_block = (result * mine_filled).astype(jnp.bfloat16)[None]

    heads = jnp.concatenate([dot(hidden, up_rows, 0, 0), dot(mixed, up_rows, 0, 0)], 1)
    heads = heads.astype(jnp.bfloat16)
    bias = jnp.stack(
        [
            jnp.sum(d_pre.astype(jnp.float32), 0),
            jnp.pad(jnp.sum(up_rows.astype(jnp.float32), 0), (0, half - out)),
        ]
    ).astype(jnp.bfloat16)
    pad = 16
    bias = jnp.pad(bias, ((0, pad - CORES), (0, 0)))
    per_y = half // Y
    sums = []
    for by in range(Y):
        piece = lax.dynamic_slice_in_dim(heads, ((at_y - by) % Y) * per_y, per_y, 0)
        piece = jnp.concatenate([d_pre, piece, bias], 0)
        sums.append(piece if by == 0 else shift(piece, "y", Y, -by))
    extra = paired([piece[span:].astype(jnp.float32) for piece in sums]).astype(jnp.bfloat16)
    d_all = jnp.concatenate([piece[:span] for piece in sums], 0)
    grads = [
        dot(feats, d_all, 1, 0).astype(jnp.bfloat16).reshape(Z, 2 * width, half)
        for feats in (feats_mine, feats_other)
    ]
    per_z = per_y // Z
    spare = 2 * width - per_z
    heads = extra[:per_y].reshape(Z, per_z, half)
    bias = jnp.broadcast_to(extra[None, per_y : per_y + 8], (Z, 8, half))
    sums = exchange(jnp.concatenate([*grads, heads, bias], 1), "z")
    sums = jnp.sum(sums.astype(jnp.float32), 0)
    sums = jnp.sum(to_all(sums, "rep", REPS), 0)
    grads_mine, grads_other = sums[: 2 * width], sums[2 * width : 4 * width]
    heads = sums[4 * width : 4 * width + per_z]
    bias = sums[4 * width + per_z :]
    grads_other = swap(jnp.concatenate([grads_other, bias], 0))
    bias_other = grads_other[2 * width]
    grads_other = grads_other[: 2 * width]
    heads = to_all(heads, chips, CHIPS).reshape(half, 2 * out)
    heads_other = swap(heads)

    def ordered(mine, other, axis):
        return jnp.concatenate(
            [jnp.where(first, mine, other), jnp.where(first, other, mine)], axis
        )

    grads = ordered(grads_mine, grads_other, 1)
    heads = ordered(heads, heads_other, 0)
    return (
        out_block,
        grads[:width],
        grads[width:],
        ordered(bias[0], bias_other, 0),
        heads[:, :out],
        heads[:, out:],
        bias[1, :out],
    )


def solution(mesh):
    fine = Mesh(mesh.devices.reshape(Y, Z, CORES, REPS), ("y", "z", "core", "rep"))
    feat = ("y", "z", "core")
    placed = (
        P(feat, "rep"),
        P("rep", None, None),
        P("rep", None, None, None, None),
        P("rep", None, None, None),
        P("rep", None),
        P(feat, None),
        P(feat, None),
        P(),
        P(),
        P(),
        P(),
        P("rep", feat, None),
    )
    return jax.shard_map(
        on_device,
        mesh=fine,
        in_specs=placed,
        out_specs=(P("rep", feat, None), P(feat, None), P(feat, None), P(), P(), P(), P()),
        check_vma=False,
    )
```

time: 131 us -> 120 us (0.916)
  blocking collectives: 40.2 us -> 0 us
  starting transfers between devices: 24.7 us -> 43.1 us
  waiting for transfers between devices: 43.1 us -> 53.1 us
  matrix products: 12.1 us -> 3.92 us
  Pallas kernels: 0 us -> 7.39 us
  other arithmetic: 2.98 us -> 4.79 us
    all_to_all x3 -> x0, blocking collectives: 40.2 us -> none  [exchange(): return lax.all_to_all(value, axes, 0, 0, tiled=True)]
    ppermute x4 -> x11, waiting for transfers between devices: 3.46 us -> 16.2 us  [the longest x6 14.9 us: shift(): lax.ppermute(value, axis, [(i, (i + by) % count) for i in range(count)])]
    ppermute x4 -> x11, starting transfers between devices: 7.45 us -> 18.6 us  [the longest x5 12 us: swap(): return lax.ppermute(value, 'core', SWAP)]
    dot_general x14 -> x15, matrix products: 12.1 us -> 3.92 us  [the longest x14 3.25 us: dot(): lax.dot_general(left, right, (((left_dim,), (right_dim,)), ((), ())), pre...]
    pallas_call x0 -> x1, Pallas kernels: none -> 7.39 us  [gather_rows(): pl.pallas_call(functools.partial(gather_kernel, per_step=per_step), out_s...]
    all_to_all x3 -> x4, starting transfers between devices: 17.2 us -> 24.5 us  [exchange(): return lax.all_to_all(value, axes, 0, 0, tiled=True)]
    all_to_all x3 -> x4, waiting for transfers between devices: 39.6 us -> 36.9 us  [exchange(): return lax.all_to_all(value, axes, 0, 0, tiled=True)]
    reshape x4 -> x1, local copies, waits for them, and re-layouts: 2.1 us -> 0.01 us  [on_device(): heads = extra[:per_y].reshape(Z, per_z, half)]
  transfers between devices with their start and end apart: 7 -> 15, of which waited for: 6 -> 11; matrix products, arithmetic and copies ran while one was open for 4% -> 5% of each run, Pallas kernels for 0% -> 0%
where the time goes in v2:
time: 120 us; the launch traced here: 119 us
  waiting for transfers between devices  53.1 us (44%)
  starting transfers between devices  43.1 us (36%)
  Pallas kernels  7.39 us (6%)
  other arithmetic  4.79 us (4%)
  local copies, waits for them, and re-layouts  4.49 us (4%)
  matrix products  3.92 us (3%)
  between operations  2.33 us (2%)
    all_to_all x4, waiting for transfers between devices, exchange(): return lax.all_to_all(value, axes, 0, 0, tiled=True)  36.9 us
    all_to_all x4, starting transfers between devices, exchange(): return lax.all_to_all(value, axes, 0, 0, tiled=True)  24.5 us
    ppermute x6, waiting for transfers between devices, shift(): lax.ppermute(value, axis, [(i, (i + by) % count) for i in range(count)])  14.9 us
    ppermute x5, starting transfers between devices, swap(): return lax.ppermute(value, 'core', SWAP)  12 us
    pallas_call x1, Pallas kernels, gather_rows(): pl.pallas_call(functools.partial(gather_kernel, per_step=per_step), out_s...  7.39 us
    ppermute x6, starting transfers between devices, shift(): lax.ppermute(value, axis, [(i, (i + by) % count) for i in range(count)])  6.6 us
    dot_general x14, matrix products, dot(): lax.dot_general(left, right, (((left_dim,), (right_dim,)), ((), ())), pre...  3.25 us
  transfers between devices with their start and end apart: 15, of which 11 were waited for; matrix products, arithmetic and copies ran while one was open for 5% of the time, Pallas kernels for 0%

profile of v2, /device:TPU:1, one launch (start us, length us, event | category | flops | bytes accessed | tf_op | source)
XLA Modules:
  0.0 119.1 jit_solution(15352439687421065749)
XLA Ops:
  0.7 0.8 copy.26
  1.5 0.7 reshape_squeeze.3.neighbours
  2.2 0.6 pad_add_fusion.place
  2.8 7.4 %gather_rows.1 = bf16[8,32,1536]{2,1,0:T(8,128)(2,1)} custom-call(s32[256]{0:T(256)} %reshape_squeeze.3.neighbours, s32[32]{0:T(128)} %bitcast.62, s32[2]{0:T(128)} %pad_add_fusion.place, bf16[16,32768]{1,0:T(8,128)(2,1)} %feats.1, bf16[32,8,128,128]{3,2,1,0:T(8,128)(2,1)} %bitcast.52, bf16[16,512]{1,0:T(8,128)(2,1)} %own.1, bf16[16,512]{1,0:T(8,128)(2,1)} %near.1), custom_call_target="tpu_custom_call" | custom-call | flops 134217728 | bytes 9437184 | tf_op jit(solution)/shard_map/gather_rows/pallas_call | solution.py:95
  10.2 9.0 %all-to-all-start = ((bf16[8,32,1536]{2,1,0:T(8,128)(2,1)}), bf16[8,32,1536]{2,1,0:T(8,128)(2,1)S(1)}, u32[]{:S(2)}, u32[]{:S(2)}) async-start(bf16[8,32,1536]{2,1,0:T(8,128)(2,1)} %gather_rows.1), calls=%async_computation | async-start | bytes 1572864 | tf_op jit(solution)/shard_map/all_to_all | solution.py:27
  19.2 1.0 collective-permute-start.5
  20.4 0.7 convolution_convert_fusion.5
  21.7 21.1 %all-to-all-done = bf16[8,32,1536]{2,1,0:T(8,128)(2,1)S(1)} async-done(((bf16[8,32,1536]{2,1,0:T(8,128)(2,1)}), bf16[8,32,1536]{2,1,0:T(8,128)(2,1)S(1)}, u32[]{:S(2)}, u32[]{:S(2)}) %all-to-all-start) | async-done | bytes 786464 | tf_op jit(solution)/shard_map/all_to_all | solution.py:27
  42.8 0.6 collective-permute-start
  43.4 0.2 convolution_convert_fusion.2
  43.6 0.2 fusion.12
  43.8 0.4 fusion.7
  44.1 1.0 collective-permute-done
  45.1 0.4 fusion
  45.5 2.8 %collective-permute-start.3 = (bf16[256,256]{1,0:T(8,128)(2,1)S(1)}, bf16[256,256]{1,0:T(8,128)(2,1)S(1)}, u32[]{:S(2)}, u32[]{:S(2)}) collective-permute-start(bf16[256,256]{1,0:T(8,128)(2,1)S(1)} %get-tuple-element.12), channel_id=1, source_target_pairs={{0,192},{64,0},{128,64},{192,128},{1,193},{65,1},{129,65},{193,129... | collective-permute-start | bytes 393224 | tf_op jit(solution)/shard_map/ppermute | solution.py:39
  48.3 0.3 collective-permute-start.2
  48.7 0.7 collective-permute-start.1
  49.4 0.2 fusion.14
  49.6 3.9 %collective-permute-done.3 = bf16[256,256]{1,0:T(8,128)(2,1)S(1)} collective-permute-done((bf16[256,256]{1,0:T(8,128)(2,1)S(1)}, bf16[256,256]{1,0:T(8,128)(2,1)S(1)}, u32[]{:S(2)}, u32[]{:S(2)}) %collective-permute-start.3) | collective-permute-done | bytes 131104 | tf_op jit(solution)/shard_map/ppermute | solution.py:39
  53.5 0.7 collective-permute-done.2
  54.2 3.8 %collective-permute-done.1 = bf16[256,256]{1,0:T(8,128)(2,1)S(1)} collective-permute-done((bf16[256,256]{1,0:T(8,128)(2,1)S(1)}, bf16[256,256]{1,0:T(8,128)(2,1)S(1)}, u32[]{:S(2)}, u32[]{:S(2)}) %collective-permute-start.1) | collective-permute-done | bytes 131104 | tf_op jit(solution)/shard_map/ppermute | solution.py:39
  58.5 0.2 convolution_convert_fusion.7
  58.7 0.3 fusion.54
  59.0 0.2 convolution_convert_fusion.6
  59.5 2.7 %collective-permute-start.6 = (bf16[336,256]{1,0:T(8,128)(2,1)S(1)}, bf16[336,256]{1,0:T(8,128)(2,1)S(1)}, u32[]{:S(2)}, u32[]{:S(2)}) collective-permute-start(bf16[336,256]{1,0:T(8,128)(2,1)S(1)} %get-tuple-element.16), channel_id=1, source_target_pairs={{0,192},{64,0},{128,64},{192,128},{1,193},{65,1},{129,65},{193,129... | collective-permute-start | bytes 516104 | tf_op jit(solution)/shard_map/ppermute | solution.py:39
  62.1 4.0 %collective-permute-done.8 = bf16[336,256]{1,0:T(8,128)(2,1)S(1)} collective-permute-done((bf16[336,256]{1,0:T(8,128)(2,1)S(1)}, bf16[336,256]{1,0:T(8,128)(2,1)S(1)}, u32[]{:S(2)}, u32[]{:S(2)}) %collective-permute-start.8) | collective-permute-done | bytes 172064 | tf_op jit(solution)/shard_map/ppermute | solution.py:39
  66.1 2.4 %collective-permute-done.7 = bf16[336,256]{1,0:T(8,128)(2,1)S(1)} collective-permute-done((bf16[336,256]{1,0:T(8,128)(2,1)S(1)}, bf16[336,256]{1,0:T(8,128)(2,1)S(1)}, u32[]{:S(2)}, u32[]{:S(2)}) %collective-permute-start.7) | collective-permute-done | bytes 172064 | tf_op jit(solution)/shard_map/ppermute | solution.py:39
  68.6 0.3 convolution_convert_fusion.1
  68.9 0.3 convolution_convert_fusion
  69.3 0.7 pad_maximum_fusion.1
  70.0 3.4 %all-to-all-start.1 = ((bf16[8,80,256]{2,1,0:T(8,128)(2,1)}), bf16[8,80,256]{2,1,0:T(8,128)(2,1)S(1)}, u32[]{:S(2)}, u32[]{:S(2)}) async-start(bf16[8,80,256]{2,1,0:T(8,128)(2,1)} %pad_maximum_fusion.1), calls=%async_computation.1 | async-start | bytes 655360 | tf_op jit(solution)/shard_map/all_to_all | solution.py:27
  73.8 2.7 %collective-permute-start.4 = (f32[128,128]{1,0:T(8,128)S(1)}, f32[128,128]{1,0:T(8,128)S(1)}, u32[]{:S(2)}, u32[]{:S(2)}) collective-permute-start(f32[128,128]{1,0:T(8,128)S(1)} %slice_select_fusion), channel_id=1, source_target_pairs={{0,4},{4,0},{1,5},{5,1},{2,6},{6,2},{3,7},{7,3},{8,12},{12,8},{9,1... | collective-permute-start | bytes 196616 | tf_op jit(solution)/shard_map/ppermute | solution.py:35
  76.5 6.8 %all-to-all-done.1 = bf16[8,80,256]{2,1,0:T(8,128)(2,1)S(1)} async-done(((bf16[8,80,256]{2,1,0:T(8,128)(2,1)}), bf16[8,80,256]{2,1,0:T(8,128)(2,1)S(1)}, u32[]{:S(2)}, u32[]{:S(2)}) %all-to-all-start.1) | async-done | bytes 327712 | tf_op jit(solution)/shard_map/all_to_all | solution.py:27
  83.4 0.7 broadcast_in_dim.10
  84.2 4.0 %all-to-all-start.2 = ((f32[4,80,256]{2,1,0:T(8,128)}), f32[4,80,256]{2,1,0:T(8,128)S(1)}, u32[]{:S(2)}, u32[]{:S(2)}) async-start(f32[4,80,256]{2,1,0:T(8,128)} %broadcast_in_dim.10), calls=%async_computation.2 | async-start | bytes 655360 | tf_op jit(solution)/shard_map/all_to_all | solution.py:27
  88.2 0.6 fusion.53
  90.1 0.6 fusion.23
  90.7 3.3 %all-to-all-done.2 = f32[4,80,256]{2,1,0:T(8,128)S(1)} async-done(((f32[4,80,256]{2,1,0:T(8,128)}), f32[4,80,256]{2,1,0:T(8,128)S(1)}, u32[]{:S(2)}, u32[]{:S(2)}) %all-to-all-start.2) | async-done | bytes 327712 | tf_op jit(solution)/shard_map/all_to_all | solution.py:27
  94.1 0.7 broadcast_in_dim.11
  94.8 8.0 %all-to-all-start.3 = ((f32[32,8,256]{2,1,0:T(8,128)}), f32[32,8,256]{2,1,0:T(8,128)S(1)}, u32[]{:S(2)}, u32[]{:S(2)}) async-start(f32[32,8,256]{2,1,0:T(8,128)} %broadcast_in_dim.11), calls=%async_computation.3 | async-start | bytes 524288 | tf_op jit(solution)/shard_map/all_to_all | solution.py:27
  102.9 3.3 %collective-permute-start.9 = (f32[40,256]{1,0:T(8,128)S(1)}, f32[40,256]{1,0:T(8,128)S(1)}, u32[]{:S(2)}, u32[]{:S(2)}) collective-permute-start(f32[40,256]{1,0:T(8,128)S(1)} %pad_maximum_fusion.15), channel_id=1, source_target_pairs={{0,4},{4,0},{1,5},{5,1},{2,6},{6,2},{3,7},{7,3},{8,12},{12,8},{9,1... | collective-permute-start | bytes 122888 | tf_op jit(solution)/shard_map/ppermute | solution.py:35
  106.2 0.5 slice_bitcast_fusion.1
  106.7 0.4 collective-permute-done.9
  107.0 5.6 %all-to-all-done.3 = f32[32,8,256]{2,1,0:T(8,128)S(1)} async-done(((f32[32,8,256]{2,1,0:T(8,128)}), f32[32,8,256]{2,1,0:T(8,128)S(1)}, u32[]{:S(2)}, u32[]{:S(2)}) %all-to-all-start.3) | async-done | bytes 262176 | tf_op jit(solution)/shard_map/all_to_all | solution.py:27
  112.6 4.4 %collective-permute-start.10 = (f32[256,256]{1,0:T(8,128)S(1)}, f32[256,256]{1,0:T(8,128)S(1)}, u32[]{:S(2)}, u32[]{:S(2)}) collective-permute-start(f32[256,256]{1,0:T(8,128)S(1)} %bitcast.56), channel_id=1, source_target_pairs={{0,4},{4,0},{1,5},{5,1},{2,6},{6,2},{3,7},{7,3},{8,12},{12,8},{9,1... | collective-permute-start | bytes 786440 | tf_op jit(solution)/shard_map/ppermute | solution.py:35
  117.0 0.6 pad_maximum_fusion.17
  117.6 0.6 pad_maximum_fusion.16
  118.3 0.8 pad_maximum_fusion.5
  (58 shorter events, 2.0 us)
Async XLA Ops:
  0.6 19.8 %copy-start = (bf16[1,32,128,128]{3,2,1,0:T(8,128)(2,1)S(1)}, bf16[1,32,128,128]{3,2,1,0:T(8,128)(2,1)}, u32[]{:S(2)}) copy-start(bf16[1,32,128,128]{3,2,1,0:T(8,128)(2,1)} %param.15) | copy-start | bytes 3145732
  0.6 19.6 %copy-start.4 = (s32[1,32]{1,0:T(1,128)S(1)}, s32[1,32]{1,0:T(1,128)}, u32[]{:S(2)}) copy-start(s32[1,32]{1,0:T(1,128)} %param.16) | copy-start | bytes 388
  0.7 18.5 %copy-start.3 = (bf16[1,128,128]{2,1,0:T(8,128)(2,1)S(1)}, bf16[1,128,128]{2,1,0:T(8,128)(2,1)}, u32[]{:S(2)}) copy-start(bf16[1,128,128]{2,1,0:T(8,128)(2,1)} %param.23) | copy-start | bytes 98308
  0.7 20.6 %copy-start.6 = (f32[512]{0:T(512)S(1)}, f32[512]{0:T(512)}, u32[]{:S(2)}) copy-start(f32[512]{0:T(512)} %param.19) | copy-start | bytes 6148
  0.7 42.7 %copy-start.1 = (bf16[512,128]{1,0:T(8,128)(2,1)S(1)}, bf16[512,128]{1,0:T(8,128)(2,1)}, u32[]{:S(2)}) copy-start(bf16[512,128]{1,0:T(8,128)(2,1)} %param.21) | copy-start | bytes 393220
  2.8 55.9 %copy-start.2 = (bf16[512,128]{1,0:T(8,128)(2,1)S(1)}, bf16[512,128]{1,0:T(8,128)(2,1)}, u32[]{:S(2)}) copy-start(bf16[512,128]{1,0:T(8,128)(2,1)} %param.20) | copy-start | bytes 393220
  10.2 32.6 %all-to-all-start = ((bf16[8,32,1536]{2,1,0:T(8,128)(2,1)}), bf16[8,32,1536]{2,1,0:T(8,128)(2,1)S(1)}, u32[]{:S(2)}, u32[]{:S(2)}) async-start(bf16[8,32,1536]{2,1,0:T(8,128)(2,1)} %gather_rows.1), calls=%async_computation | async-start | bytes 1572864 | tf_op jit(solution)/shard_map/all_to_all | solution.py:27
  19.2 2.2 %collective-permute-start.5 = (bf16[128,128]{1,0:T(8,128)(2,1)S(1)}, bf16[128,128]{1,0:T(8,128)(2,1)S(1)}, u32[]{:S(2)}, u32[]{:S(2)}) collective-permute-start(bf16[128,128]{1,0:T(8,128)(2,1)S(1)} %bitcast.59), channel_id=1, source_target_pairs={{0,4},{4,0},{1,5},{5,1},{2,6},{6,2},{3,7},{7,3},{8,12},{12,8},{9,1... | collective-permute-start | bytes 98312 | tf_op jit(solution)/shard_map/ppermute | solution.py:35
  42.8 2.3 %collective-permute-start = (bf16[256,1280]{1,0:T(8,128)(2,1)S(1)}, bf16[256,1280]{1,0:T(8,128)(2,1)S(1)}, u32[]{:S(2)}, u32[]{:S(2)}) collective-permute-start(bf16[256,1280]{1,0:T(8,128)(2,1)S(1)} %slice.170), channel_id=1, source_target_pairs={{0,4},{4,0},{1,5},{5,1},{2,6},{6,2},{3,7},{7,3},{8,12},{12,8},{9,1... | collective-permute-start | bytes 1966088 | tf_op jit(solution)/shard_map/ppermute | solution.py:35
  45.5 44.6 %copy-start.5 = (f32[128]{0:T(128)S(1)}, f32[128]{0:T(128)}, u32[]{:S(2)}) copy-start(f32[128]{0:T(128)} %param.22) | copy-start | bytes 1540
  45.5 8.0 %collective-permute-start.3 = (bf16[256,256]{1,0:T(8,128)(2,1)S(1)}, bf16[256,256]{1,0:T(8,128)(2,1)S(1)}, u32[]{:S(2)}, u32[]{:S(2)}) collective-permute-start(bf16[256,256]{1,0:T(8,128)(2,1)S(1)} %get-tuple-element.12), channel_id=1, source_target_pairs={{0,192},{64,0},{128,64},{192,128},{1,193},{65,1},{129,65},{193,129... | collective-permute-start | bytes 393224 | tf_op jit(solution)/shard_map/ppermute | solution.py:39
  48.3 5.9 %collective-permute-start.2 = (bf16[256,256]{1,0:T(8,128)(2,1)S(1)}, bf16[256,256]{1,0:T(8,128)(2,1)S(1)}, u32[]{:S(2)}, u32[]{:S(2)}) collective-permute-start(bf16[256,256]{1,0:T(8,128)(2,1)S(1)} %get-tuple-element.13), channel_id=1, source_target_pairs={{0,128},{64,192},{128,0},{192,64},{1,129},{65,193},{129,1},{193,65... | collective-permute-start | bytes 393224 | tf_op jit(solution)/shard_map/ppermute | solution.py:39
  48.7 9.4 %collective-permute-start.1 = (bf16[256,256]{1,0:T(8,128)(2,1)S(1)}, bf16[256,256]{1,0:T(8,128)(2,1)S(1)}, u32[]{:S(2)}, u32[]{:S(2)}) collective-permute-start(bf16[256,256]{1,0:T(8,128)(2,1)S(1)} %get-tuple-element.11), channel_id=1, source_target_pairs={{0,64},{64,128},{128,192},{192,0},{1,65},{65,129},{129,193},{193,1... | collective-permute-start | bytes 393224 | tf_op jit(solution)/shard_map/ppermute | solution.py:39
  59.4 6.7 %collective-permute-start.8 = (bf16[336,256]{1,0:T(8,128)(2,1)S(1)}, bf16[336,256]{1,0:T(8,128)(2,1)S(1)}, u32[]{:S(2)}, u32[]{:S(2)}) collective-permute-start(bf16[336,256]{1,0:T(8,128)(2,1)S(1)} %get-tuple-element.15), channel_id=1, source_target_pairs={{0,64},{64,128},{128,192},{192,0},{1,65},{65,129},{129,193},{193,1... | collective-permute-start | bytes 516104 | tf_op jit(solution)/shard_map/ppermute | solution.py:39
  59.5 6.6 %collective-permute-start.6 = (bf16[336,256]{1,0:T(8,128)(2,1)S(1)}, bf16[336,256]{1,0:T(8,128)(2,1)S(1)}, u32[]{:S(2)}, u32[]{:S(2)}) collective-permute-start(bf16[336,256]{1,0:T(8,128)(2,1)S(1)} %get-tuple-element.16), channel_id=1, source_target_pairs={{0,192},{64,0},{128,64},{192,128},{1,193},{65,1},{129,65},{193,129... | collective-permute-start | bytes 516104 | tf_op jit(solution)/shard_map/ppermute | solution.py:39
  62.1 6.4 %collective-permute-start.7 = (bf16[336,256]{1,0:T(8,128)(2,1)S(1)}, bf16[336,256]{1,0:T(8,128)(2,1)S(1)}, u32[]{:S(2)}, u32[]{:S(2)}) collective-permute-start(bf16[336,256]{1,0:T(8,128)(2,1)S(1)} %get-tuple-element.14), channel_id=1, source_target_pairs={{0,128},{64,192},{128,0},{192,64},{1,129},{65,193},{129,1},{193,65... | collective-permute-start | bytes 516104 | tf_op jit(solution)/shard_map/ppermute | solution.py:39
  70.0 13.4 %all-to-all-start.1 = ((bf16[8,80,256]{2,1,0:T(8,128)(2,1)}), bf16[8,80,256]{2,1,0:T(8,128)(2,1)S(1)}, u32[]{:S(2)}, u32[]{:S(2)}) async-start(bf16[8,80,256]{2,1,0:T(8,128)(2,1)} %pad_maximum_fusion.1), calls=%async_computation.1 | async-start | bytes 655360 | tf_op jit(solution)/shard_map/all_to_all | solution.py:27
  73.8 16.2 %collective-permute-start.4 = (f32[128,128]{1,0:T(8,128)S(1)}, f32[128,128]{1,0:T(8,128)S(1)}, u32[]{:S(2)}, u32[]{:S(2)}) collective-permute-start(f32[128,128]{1,0:T(8,128)S(1)} %slice_select_fusion), channel_id=1, source_target_pairs={{0,4},{4,0},{1,5},{5,1},{2,6},{6,2},{3,7},{7,3},{8,12},{12,8},{9,1... | collective-permute-start | bytes 196616 | tf_op jit(solution)/shard_map/ppermute | solution.py:35
  84.2 9.9 %all-to-all-start.2 = ((f32[4,80,256]{2,1,0:T(8,128)}), f32[4,80,256]{2,1,0:T(8,128)S(1)}, u32[]{:S(2)}, u32[]{:S(2)}) async-start(f32[4,80,256]{2,1,0:T(8,128)} %broadcast_in_dim.10), calls=%async_computation.2 | async-start | bytes 655360 | tf_op jit(solution)/shard_map/all_to_all | solution.py:27
  94.8 17.8 %all-to-all-start.3 = ((f32[32,8,256]{2,1,0:T(8,128)}), f32[32,8,256]{2,1,0:T(8,128)S(1)}, u32[]{:S(2)}, u32[]{:S(2)}) async-start(f32[32,8,256]{2,1,0:T(8,128)} %broadcast_in_dim.11), calls=%async_computation.3 | async-start | bytes 524288 | tf_op jit(solution)/shard_map/all_to_all | solution.py:27
  102.9 4.2 %collective-permute-start.9 = (f32[40,256]{1,0:T(8,128)S(1)}, f32[40,256]{1,0:T(8,128)S(1)}, u32[]{:S(2)}, u32[]{:S(2)}) collective-permute-start(f32[40,256]{1,0:T(8,128)S(1)} %pad_maximum_fusion.15), channel_id=1, source_target_pairs={{0,4},{4,0},{1,5},{5,1},{2,6},{6,2},{3,7},{7,3},{8,12},{12,8},{9,1... | collective-permute-start | bytes 122888 | tf_op jit(solution)/shard_map/ppermute | solution.py:35
  112.6 5.6 %collective-permute-start.10 = (f32[256,256]{1,0:T(8,128)S(1)}, f32[256,256]{1,0:T(8,128)S(1)}, u32[]{:S(2)}, u32[]{:S(2)}) collective-permute-start(f32[256,256]{1,0:T(8,128)S(1)} %bitcast.56), channel_id=1, source_target_pairs={{0,4},{4,0},{1,5},{5,1},{2,6},{6,2},{3,7},{7,3},{8,12},{12,8},{9,1... | collective-permute-start | bytes 786440 | tf_op jit(solution)/shard_map/ppermute | solution.py:35

commit v3 on v2

--- a/solution.py
+++ b/solution.py
@@ -48,19 +48,20 @@
     return paired(terms)
 
 
-def gather_kernel(neighbours, owners, place, feats, edges, own, near, out, *, per_step):
+def gather_kernel(neighbours, owners, feats, edges, own, near, out, *, per_step):
     step = pl.program_id(0)
     width = feats.shape[0]
     fan, rows = edges.shape[1], edges.shape[-1]
     layer_rows = Y * CORES * rows
     half = own.shape[1] // CORES
+    at_y, at_core = lax.axis_index("y"), lax.axis_index("core")
 
     @pl.when(step == 0)
     def _():
         out[:, :, half : half + layer_rows] = jnp.zeros((Z, 2 * width, layer_rows), out.dtype)
         for c in range(CORES):
 
-            @pl.when(place[1] == c)
+            @pl.when(at_core == c)
             def _(c=c):
                 kept, given = c * half, (1 - c) * half
                 for z in range(Z):
@@ -71,23 +72,23 @@
 
     for i in range(per_step):
         block = step * per_step + i
-        starts = [pl.multiple_of(neighbours[block * fan + k] * rows, rows) for k in range(fan)]
+        starts = [pl.multiple_of(neighbours[k, block] * rows, rows) for k in range(fan)]
         total = lax.dot_general(
             jnp.concatenate([feats[:, pl.ds(start, rows)] for start in starts], 1),
             jnp.concatenate([edges[i, k] for k in range(fan)], 1),
             (((1,), (1,)), ((), ())),
             preferred_element_type=jnp.float32,
         )
-        owner = owners[block]
+        owner = owners[0, block]
         core = owner & (CORES - 1)
         z = lax.shift_right_logical(owner, 1) & (Z - 1)
-        y = (lax.shift_right_logical(owner, 4) - place[0]) & (Y - 1)
+        y = (lax.shift_right_logical(owner, 4) - at_y) & (Y - 1)
         lane = pl.multiple_of(half + (y * CORES + core) * rows, rows)
         out[z, :width, pl.ds(lane, rows)] = feats[:, pl.ds(pl.multiple_of(block * rows, rows), rows)]
         out[z, width:, pl.ds(lane, rows)] = total.astype(out.dtype)
 
 
-def gather_rows(neighbours, owners, place, feats, edges, own, near):
+def gather_rows(neighbours, owners, feats, edges, own, near):
     blocks, fan, rows, _ = edges.shape
     width = feats.shape[0]
     columns = Y * CORES * rows + own.shape[1]
@@ -96,7 +97,7 @@
         functools.partial(gather_kernel, per_step=per_step),
         out_shape=jax.ShapeDtypeStruct((Z, 2 * width, columns), feats.dtype),
         grid_spec=pltpu.PrefetchScalarGridSpec(
-            num_scalar_prefetch=3,
+            num_scalar_prefetch=2,
             grid=(blocks // per_step,),
             in_specs=[
                 pl.BlockSpec(feats.shape, lambda i, *_: (0, 0)),
@@ -113,7 +114,41 @@
             transcendentals=0,
         ),
         name="gather_rows",
-    )(neighbours.reshape(-1), owners, place, feats, edges, own, near)
+    )(neighbours, owners, feats, edges, own, near)
+
+
+def grads_kernel(*refs):
+    pieces, extras, (mine, other, out) = refs[:Y], refs[Y : 2 * Y], refs[2 * Y :]
+    half = out.shape[2]
+    rows = mine.shape[0] // Z
+    layer_rows = mine.shape[1] - 2 * half
+    d_all = jnp.concatenate([piece[...] for piece in pieces], 0)
+    for i, feats in enumerate((mine[:, half : half + layer_rows], other[:, :layer_rows])):
+        grads = jnp.dot(feats, d_all, preferred_element_type=jnp.float32).astype(out.dtype)
+        for z in range(Z):
+            out[z, i * rows : (i + 1) * rows] = grads[z * rows : (z + 1) * rows]
+    extra = paired([piece[...].astype(jnp.float32) for piece in extras])
+    per = half // CHIPS
+    bias = extra[Z * per : Z * per + 8]
+    for z in range(Z):
+        block = jnp.concatenate([extra[z * per : (z + 1) * per], bias], 0)
+        out[z, CORES * rows :] = block.astype(out.dtype)
+
+
+def grad_parts(pieces, extras, mine, other):
+    half = pieces[0].shape[1]
+    rows = CORES * mine.shape[0] // Z + half // CHIPS + 8
+    return pl.pallas_call(
+        grads_kernel,
+        out_shape=jax.ShapeDtypeStruct((Z, rows, half), pieces[0].dtype),
+        compiler_params=pltpu.CompilerParams(vmem_limit_bytes=32 * 1024 * 1024),
+        cost_estimate=pl.CostEstimate(
+            flops=4 * mine.shape[0] * (mine.shape[1] - 2 * half) * half,
+            bytes_accessed=2 * (mine.size + other.size + Y * pieces[0].size),
+            transcendentals=0,
+        ),
+        name="grad_parts",
+    )(*pieces, *extras, mine, other)
 
 
 def on_device(
@@ -145,9 +180,8 @@
 
     span = CORES * rows
     sent = gather_rows(
-        neighbour_blocks[0],
-        owners[0],
-        jnp.stack([at_y, core]).astype(jnp.int32),
+        neighbour_blocks[0].T,
+        owners,
         node_feats,
         edge_weights[0],
         self_weight,
@@ -211,24 +245,17 @@
     pad = 16
     bias = jnp.pad(bias, ((0, pad - CORES), (0, 0)))
     per_y = half // Y
-    sums = []
+    pieces, extras = [d_pre], []
+    for by in range(1, Y):
+        pieces.append(shift(d_pre, "y", Y, -by))
     for by in range(Y):
         piece = lax.dynamic_slice_in_dim(heads, ((at_y - by) % Y) * per_y, per_y, 0)
-        piece = jnp.concatenate([d_pre, piece, bias], 0)
-        sums.append(piece if by == 0 else shift(piece, "y", Y, -by))
-    extra = paired([piece[span:].astype(jnp.float32) for piece in sums]).astype(jnp.bfloat16)
-    d_all = jnp.concatenate([piece[:span] for piece in sums], 0)
-    grads = [
-        dot(feats, d_all, 1, 0).astype(jnp.bfloat16).reshape(Z, 2 * width, half)
-        for feats in (feats_mine, feats_other)
-    ]
+        piece = jnp.concatenate([piece, bias], 0)
+        extras.append(piece if by == 0 else shift(piece, "y", Y, -by))
     per_z = per_y // Z
-    spare = 2 * width - per_z
-    heads = extra[:per_y].reshape(Z, per_z, half)
-    bias = jnp.broadcast_to(extra[None, per_y : per_y + 8], (Z, 8, half))
-    sums = exchange(jnp.concatenate([*grads, heads, bias], 1), "z")
+    sums = exchange(grad_parts(pieces, extras, arrived, from_other), "z")
     sums = jnp.sum(sums.astype(jnp.float32), 0)
-    sums = jnp.sum(to_all(sums, "rep", REPS), 0)
+    sums = rep_sum(sums)
     grads_mine, grads_other = sums[: 2 * width], sums[2 * width : 4 * width]
     heads = sums[4 * width : 4 * width + per_z]
     bias = sums[4 * width + per_z :]

time: 120 us -> 115 us (0.958)
  waiting for transfers between devices: 53.1 us -> 47.9 us
  local copies, waits for them, and re-layouts: 4.49 us -> 2.2 us
  starting transfers between devices: 43.1 us -> 45.2 us
  other arithmetic: 4.79 us -> 3.41 us
  Pallas kernels: 7.39 us -> 8.62 us
    ppermute x6 -> x12, starting transfers between devices: 6.6 us -> 14.9 us  [shift(): lax.ppermute(value, axis, [(i, (i + by) % count) for i in range(count)])]
    all_to_all x4 -> x3, starting transfers between devices: 24.5 us -> 16.8 us  [exchange(): return lax.all_to_all(value, axes, 0, 0, tiled=True)]
    all_to_all x4 -> x3, waiting for transfers between devices: 36.9 us -> 32.5 us  [exchange(): return lax.all_to_all(value, axes, 0, 0, tiled=True)]
    ppermute x5, starting transfers between devices: 12 us -> 13.5 us  [swap(): return lax.ppermute(value, 'core', SWAP)]
    dot_general x14 -> x12, matrix products: 3.25 us -> 4.31 us  [dot(): lax.dot_general(left, right, (((left_dim,), (right_dim,)), ((), ())), pre...]
    ppermute x6 -> x12, waiting for transfers between devices: 14.9 us -> 14.1 us  [shift(): lax.ppermute(value, axis, [(i, (i + by) % count) for i in range(count)])]
  transfers between devices with their start and end apart: 15 -> 20, of which waited for: 11 -> 11; matrix products, arithmetic and copies ran while one was open for 5% -> 6% of each run, Pallas kernels for 0% -> 0%
where the time goes in v3:
time: 115 us
  waiting for transfers between devices  47.9 us (42%)
  starting transfers between devices  45.2 us (39%)
  Pallas kernels  8.62 us (7%)
  matrix products  4.98 us (4%)
  other arithmetic  3.41 us (3%)
  between operations  2.26 us (2%)
  local copies, waits for them, and re-layouts  2.2 us (2%)
    all_to_all x3, waiting for transfers between devices, exchange(): return lax.all_to_all(value, axes, 0, 0, tiled=True)  32.5 us
    all_to_all x3, starting transfers between devices, exchange(): return lax.all_to_all(value, axes, 0, 0, tiled=True)  16.8 us
    ppermute x12, starting transfers between devices, shift(): lax.ppermute(value, axis, [(i, (i + by) % count) for i in range(count)])  14.9 us
    ppermute x12, waiting for transfers between devices, shift(): lax.ppermute(value, axis, [(i, (i + by) % count) for i in range(count)])  14.1 us
    ppermute x5, starting transfers between devices, swap(): return lax.ppermute(value, 'core', SWAP)  13.5 us
    pallas_call x1, Pallas kernels, gather_rows(): pl.pallas_call(functools.partial(gather_kernel, per_step=per_step), out_s...  7.46 us
    dot_general x12, matrix products, dot(): lax.dot_general(left, right, (((left_dim,), (right_dim,)), ((), ())), pre...  4.31 us
  transfers between devices with their start and end apart: 20, of which 11 were waited for; matrix products, arithmetic and copies ran while one was open for 6% of the time, Pallas kernels for 0%

profile of v3, /device:TPU:1, one launch (start us, length us, event | category | flops | bytes accessed | tf_op | source)
XLA Modules:
  0.0 114.6 jit_solution(3104630818407588507)
XLA Ops:
  0.7 7.5 %gather_rows.1 = bf16[8,32,1536]{2,1,0:T(8,128)(2,1)} custom-call(s32[8,32]{1,0:T(8,128)} %bitcast.55, s32[1,32]{1,0:T(1,128)} %owners.1, bf16[16,32768]{1,0:T(8,128)(2,1)} %feats.1, bf16[32,8,128,128]{3,2,1,0:T(8,128)(2,1)} %bitcast.52, bf16[16,512]{1,0:T(8,128)(2,1)} %own.1, bf16[16,512]{1,0:T(8,128)(2,1)} %near.1), custom_call_target="tpu_custom_call" | custom-call | flops 134217728 | bytes 9437184 | tf_op jit(solution)/shard_map/gather_rows/pallas_call | solution.py:96
  8.2 9.0 %all-to-all-start = ((bf16[8,32,1536]{2,1,0:T(8,128)(2,1)}), bf16[8,32,1536]{2,1,0:T(8,128)(2,1)S(1)}, u32[]{:S(2)}, u32[]{:S(2)}) async-start(bf16[8,32,1536]{2,1,0:T(8,128)(2,1)} %gather_rows.1), calls=%async_computation | async-start | bytes 1572864 | tf_op jit(solution)/shard_map/all_to_all | solution.py:27
  17.2 1.0 collective-permute-start.5
  18.4 0.7 convolution_convert_fusion.3
  19.7 21.1 %all-to-all-done = bf16[8,32,1536]{2,1,0:T(8,128)(2,1)S(1)} async-done(((bf16[8,32,1536]{2,1,0:T(8,128)(2,1)}), bf16[8,32,1536]{2,1,0:T(8,128)(2,1)S(1)}, u32[]{:S(2)}, u32[]{:S(2)}) %all-to-all-start) | async-done | bytes 786464 | tf_op jit(solution)/shard_map/all_to_all | solution.py:27
  40.8 0.6 collective-permute-start
  41.6 0.2 fusion.10
  41.8 0.4 fusion.5
  42.1 1.0 collective-permute-done.refs_9_
  43.1 0.3 fusion
  43.5 2.8 %collective-permute-start.3 = (bf16[256,256]{1,0:T(8,128)(2,1)S(1)}, bf16[256,256]{1,0:T(8,128)(2,1)S(1)}, u32[]{:S(2)}, u32[]{:S(2)}) collective-permute-start(bf16[256,256]{1,0:T(8,128)(2,1)S(1)} %get-tuple-element.12), channel_id=1, source_target_pairs={{0,192},{64,0},{128,64},{192,128},{1,193},{65,1},{129,65},{193,129... | collective-permute-start | bytes 393224 | tf_op jit(solution)/shard_map/ppermute | solution.py:39
  46.3 0.4 collective-permute-start.2
  46.7 0.7 collective-permute-start.1
  47.4 0.2 fusion.12
  47.5 3.9 %collective-permute-done.3 = bf16[256,256]{1,0:T(8,128)(2,1)S(1)} collective-permute-done((bf16[256,256]{1,0:T(8,128)(2,1)S(1)}, bf16[256,256]{1,0:T(8,128)(2,1)S(1)}, u32[]{:S(2)}, u32[]{:S(2)}) %collective-permute-start.3) | collective-permute-done | bytes 131104 | tf_op jit(solution)/shard_map/ppermute | solution.py:39
  51.5 0.7 collective-permute-done.2
  52.2 3.8 %collective-permute-done.1 = bf16[256,256]{1,0:T(8,128)(2,1)S(1)} collective-permute-done((bf16[256,256]{1,0:T(8,128)(2,1)S(1)}, bf16[256,256]{1,0:T(8,128)(2,1)S(1)}, u32[]{:S(2)}, u32[]{:S(2)}) %collective-permute-start.1) | collective-permute-done | bytes 131104 | tf_op jit(solution)/shard_map/ppermute | solution.py:39
  56.5 0.2 convolution_convert_fusion.5
  56.7 0.3 fusion.50
  57.0 0.2 convolution_convert_fusion.4
  57.4 0.3 collective-permute-start.6
  57.7 3.0 %collective-permute-start.7 = (bf16[256,256]{1,0:T(8,128)(2,1)S(1)}, bf16[256,256]{1,0:T(8,128)(2,1)S(1)}, u32[]{:S(2)}, u32[]{:S(2)}) collective-permute-start(bf16[256,256]{1,0:T(8,128)(2,1)S(1)} %get-tuple-element.39.refs_0_), channel_id=1, source_target_pairs={{0,128},{64,192},{128,0},{192,64},{1,129},{65,193},{129,1},{193,65... | collective-permute-start | bytes 393224 | tf_op jit(solution)/shard_map/ppermute | solution.py:39
  60.7 1.9 %collective-permute-start.10 = (bf16[80,256]{1,0:T(8,128)(2,1)S(1)}, bf16[80,256]{1,0:T(8,128)(2,1)S(1)}, u32[]{:S(2)}, u32[]{:S(2)}) collective-permute-start(bf16[80,256]{1,0:T(8,128)(2,1)S(1)} %get-tuple-element.34), channel_id=1, source_target_pairs={{0,128},{64,192},{128,0},{192,64},{1,129},{65,193},{129,1},{193,65... | collective-permute-start | bytes 122888 | tf_op jit(solution)/shard_map/ppermute | solution.py:39
  62.5 1.4 %collective-permute-start.11 = (bf16[80,256]{1,0:T(8,128)(2,1)S(1)}, bf16[80,256]{1,0:T(8,128)(2,1)S(1)}, u32[]{:S(2)}, u32[]{:S(2)}) collective-permute-start(bf16[80,256]{1,0:T(8,128)(2,1)S(1)} %get-tuple-element.32), channel_id=1, source_target_pairs={{0,64},{64,128},{128,192},{192,0},{1,65},{65,129},{129,193},{193,1... | collective-permute-start | bytes 122888 | tf_op jit(solution)/shard_map/ppermute | solution.py:39
  63.9 0.6 fusion.49
  65.8 1.4 %collective-permute-done.10.refs_6_ = bf16[80,256]{1,0:T(8,128)(2,1)S(1)} collective-permute-done((bf16[80,256]{1,0:T(8,128)(2,1)S(1)}, bf16[80,256]{1,0:T(8,128)(2,1)S(1)}, u32[]{:S(2)}, u32[]{:S(2)}) %collective-permute-start.10) | collective-permute-done | bytes 40992 | tf_op jit(solution)/shard_map/ppermute | solution.py:39
  67.2 1.6 %collective-permute-done.11.refs_7_ = bf16[80,256]{1,0:T(8,128)(2,1)S(1)} collective-permute-done((bf16[80,256]{1,0:T(8,128)(2,1)S(1)}, bf16[80,256]{1,0:T(8,128)(2,1)S(1)}, u32[]{:S(2)}, u32[]{:S(2)}) %collective-permute-start.11) | collective-permute-done | bytes 40992 | tf_op jit(solution)/shard_map/ppermute | solution.py:39
  68.7 1.2 %grad_parts.1 = bf16[8,80,256]{2,1,0:T(8,128)(2,1)} custom-call(bf16[256,256]{1,0:T(8,128)(2,1)S(1)} %get-tuple-element.39.refs_0_, bf16[256,256]{1,0:T(8,128)(2,1)S(1)} %collective-permute-done.6.refs_1_, bf16[256,256]{1,0:T(8,128)(2,1)S(1)} %collective-permute-done.7.refs_2_, bf16[256,256]{1,0:T(8,128)(2,1)S(1)} %collective-permute-done.8.refs_3_, ...), custom_call_target="tpu_custom_call" | custom-call | flops 268435456 | bytes 1966080 | tf_op jit(solution)/shard_map/grad_parts/pallas_call | solution.py:141
  69.9 3.4 %all-to-all-start.1 = ((bf16[8,80,256]{2,1,0:T(8,128)(2,1)}), bf16[8,80,256]{2,1,0:T(8,128)(2,1)S(1)}, u32[]{:S(2)}, u32[]{:S(2)}) async-start(bf16[8,80,256]{2,1,0:T(8,128)(2,1)} %grad_parts.1), calls=%async_computation.1 | async-start | bytes 655360 | tf_op jit(solution)/shard_map/all_to_all | solution.py:27
  73.3 1.0 fusion.19
  74.4 1.0 convolution_add_fusion.2
  75.4 1.9 %collective-permute-start.4 = (f32[128,128]{1,0:T(8,128)S(1)}, f32[128,128]{1,0:T(8,128)S(1)}, u32[]{:S(2)}, u32[]{:S(2)}) collective-permute-start(f32[128,128]{1,0:T(8,128)S(1)} %slice_select_fusion), channel_id=1, source_target_pairs={{0,4},{4,0},{1,5},{5,1},{2,6},{6,2},{3,7},{7,3},{8,12},{12,8},{9,1... | collective-permute-start | bytes 196616 | tf_op jit(solution)/shard_map/ppermute | solution.py:35
  77.3 7.0 %all-to-all-done.1 = bf16[8,80,256]{2,1,0:T(8,128)(2,1)S(1)} async-done(((bf16[8,80,256]{2,1,0:T(8,128)(2,1)}), bf16[8,80,256]{2,1,0:T(8,128)(2,1)S(1)}, u32[]{:S(2)}, u32[]{:S(2)}) %all-to-all-start.1) | async-done | bytes 327712 | tf_op jit(solution)/shard_map/all_to_all | solution.py:27
  84.4 1.5 %collective-permute-start.13 = (f32[80,256]{1,0:T(8,128)S(1)}, f32[80,256]{1,0:T(8,128)S(1)}, u32[]{:S(2)}, u32[]{:S(2)}) collective-permute-start(f32[80,256]{1,0:T(8,128)S(1)} %convert_reduce_fusion), channel_id=1, source_target_pairs={{0,1},{1,2},{2,3},{3,0},{4,5},{5,6},{6,7},{7,4},{8,9},{9,10},{10,1... | collective-permute-start | bytes 245768 | tf_op jit(solution)/shard_map/ppermute | solution.py:39
  85.9 1.5 %collective-permute-start.14 = (f32[80,256]{1,0:T(8,128)S(1)}, f32[80,256]{1,0:T(8,128)S(1)}, u32[]{:S(2)}, u32[]{:S(2)}) collective-permute-start(f32[80,256]{1,0:T(8,128)S(1)} %convert_reduce_fusion), channel_id=1, source_target_pairs={{0,3},{1,0},{2,1},{3,2},{4,7},{5,4},{6,5},{7,6},{8,11},{9,8},{10,9... | collective-permute-start | bytes 245768 | tf_op jit(solution)/shard_map/ppermute | solution.py:39
  87.3 1.5 %collective-permute-start.12 = (f32[80,256]{1,0:T(8,128)S(1)}, f32[80,256]{1,0:T(8,128)S(1)}, u32[]{:S(2)}, u32[]{:S(2)}) collective-permute-start(f32[80,256]{1,0:T(8,128)S(1)} %convert_reduce_fusion), channel_id=1, source_target_pairs={{0,2},{1,3},{2,0},{3,1},{4,6},{5,7},{6,4},{7,5},{8,10},{9,11},{10,... | collective-permute-start | bytes 245768 | tf_op jit(solution)/shard_map/ppermute | solution.py:39
  88.8 0.6 fusion.21
  89.5 2.6 %collective-permute-done.12 = f32[80,256]{1,0:T(8,128)S(1)} collective-permute-done((f32[80,256]{1,0:T(8,128)S(1)}, f32[80,256]{1,0:T(8,128)S(1)}, u32[]{:S(2)}, u32[]{:S(2)}) %collective-permute-start.12) | collective-permute-done | bytes 81952 | tf_op jit(solution)/shard_map/ppermute | solution.py:39
  92.2 0.7 broadcast_in_dim.5
  92.9 4.4 %all-to-all-start.2 = ((f32[32,8,256]{2,1,0:T(8,128)}), f32[32,8,256]{2,1,0:T(8,128)S(1)}, u32[]{:S(2)}, u32[]{:S(2)}) async-start(f32[32,8,256]{2,1,0:T(8,128)} %broadcast_in_dim.5), calls=%async_computation.2 | async-start | bytes 524288 | tf_op jit(solution)/shard_map/all_to_all | solution.py:27
  97.3 4.4 %collective-permute-start.15 = (f32[40,256]{1,0:T(8,128)S(1)}, f32[40,256]{1,0:T(8,128)S(1)}, u32[]{:S(2)}, u32[]{:S(2)}) collective-permute-start(f32[40,256]{1,0:T(8,128)S(1)} %pad_maximum_fusion.9), channel_id=1, source_target_pairs={{0,4},{4,0},{1,5},{5,1},{2,6},{6,2},{3,7},{7,3},{8,12},{12,8},{9,1... | collective-permute-start | bytes 122888 | tf_op jit(solution)/shard_map/ppermute | solution.py:35
  101.7 0.5 slice_bitcast_fusion
  102.2 0.4 collective-permute-done.15
  102.6 4.3 %all-to-all-done.2 = f32[32,8,256]{2,1,0:T(8,128)S(1)} async-done(((f32[32,8,256]{2,1,0:T(8,128)}), f32[32,8,256]{2,1,0:T(8,128)S(1)}, u32[]{:S(2)}, u32[]{:S(2)}) %all-to-all-start.2) | async-done | bytes 262176 | tf_op jit(solution)/shard_map/all_to_all | solution.py:27
  106.9 5.6 %collective-permute-start.16 = (f32[256,256]{1,0:T(8,128)S(1)}, f32[256,256]{1,0:T(8,128)S(1)}, u32[]{:S(2)}, u32[]{:S(2)}) collective-permute-start(f32[256,256]{1,0:T(8,128)S(1)} %bitcast.53), channel_id=1, source_target_pairs={{0,4},{4,0},{1,5},{5,1},{2,6},{6,2},{3,7},{7,3},{8,12},{12,8},{9,1... | collective-permute-start | bytes 786440 | tf_op jit(solution)/shard_map/ppermute | solution.py:35
  112.5 0.6 pad_maximum_fusion.11
  113.1 0.6 pad_maximum_fusion.10
  113.8 0.8 pad_maximum_fusion
  (55 shorter events, 1.7 us)
Async XLA Ops:
  0.6 17.8 %copy-start = (bf16[1,32,128,128]{3,2,1,0:T(8,128)(2,1)S(1)}, bf16[1,32,128,128]{3,2,1,0:T(8,128)(2,1)}, u32[]{:S(2)}) copy-start(bf16[1,32,128,128]{3,2,1,0:T(8,128)(2,1)} %param.15) | copy-start | bytes 3145732
  0.7 17.6 %copy-start.4 = (s32[1,32]{1,0:T(1,128)S(1)}, s32[1,32]{1,0:T(1,128)}, u32[]{:S(2)}) copy-start(s32[1,32]{1,0:T(1,128)} %owners.1) | copy-start | bytes 388
  0.7 16.5 %copy-start.3 = (bf16[1,128,128]{2,1,0:T(8,128)(2,1)S(1)}, bf16[1,128,128]{2,1,0:T(8,128)(2,1)}, u32[]{:S(2)}) copy-start(bf16[1,128,128]{2,1,0:T(8,128)(2,1)} %param.23) | copy-start | bytes 98308
  0.7 18.6 %copy-start.6 = (f32[512]{0:T(512)S(1)}, f32[512]{0:T(512)}, u32[]{:S(2)}) copy-start(f32[512]{0:T(512)} %param.19) | copy-start | bytes 6148
  0.7 40.7 %copy-start.1 = (bf16[512,128]{1,0:T(8,128)(2,1)S(1)}, bf16[512,128]{1,0:T(8,128)(2,1)}, u32[]{:S(2)}) copy-start(bf16[512,128]{1,0:T(8,128)(2,1)} %param.21) | copy-start | bytes 393220
  0.7 56.0 %copy-start.2 = (bf16[512,128]{1,0:T(8,128)(2,1)S(1)}, bf16[512,128]{1,0:T(8,128)(2,1)}, u32[]{:S(2)}) copy-start(bf16[512,128]{1,0:T(8,128)(2,1)} %param.20) | copy-start | bytes 393220
  8.2 32.6 %all-to-all-start = ((bf16[8,32,1536]{2,1,0:T(8,128)(2,1)}), bf16[8,32,1536]{2,1,0:T(8,128)(2,1)S(1)}, u32[]{:S(2)}, u32[]{:S(2)}) async-start(bf16[8,32,1536]{2,1,0:T(8,128)(2,1)} %gather_rows.1), calls=%async_computation | async-start | bytes 1572864 | tf_op jit(solution)/shard_map/all_to_all | solution.py:27
  17.2 2.2 %collective-permute-start.5 = (bf16[128,128]{1,0:T(8,128)(2,1)S(1)}, bf16[128,128]{1,0:T(8,128)(2,1)S(1)}, u32[]{:S(2)}, u32[]{:S(2)}) collective-permute-start(bf16[128,128]{1,0:T(8,128)(2,1)S(1)} %bitcast.54), channel_id=1, source_target_pairs={{0,4},{4,0},{1,5},{5,1},{2,6},{6,2},{3,7},{7,3},{8,12},{12,8},{9,1... | collective-permute-start | bytes 98312 | tf_op jit(solution)/shard_map/ppermute | solution.py:35
  19.1 69.7 %copy-start.5 = (f32[128]{0:T(128)S(1)}, f32[128]{0:T(128)}, u32[]{:S(2)}) copy-start(f32[128]{0:T(128)} %param.22) | copy-start | bytes 1540
  40.8 2.3 %collective-permute-start = (bf16[256,1280]{1,0:T(8,128)(2,1)S(1)}, bf16[256,1280]{1,0:T(8,128)(2,1)S(1)}, u32[]{:S(2)}, u32[]{:S(2)}) collective-permute-start(bf16[256,1280]{1,0:T(8,128)(2,1)S(1)} %slice.138), channel_id=1, source_target_pairs={{0,4},{4,0},{1,5},{5,1},{2,6},{6,2},{3,7},{7,3},{8,12},{12,8},{9,1... | collective-permute-start | bytes 1966088 | tf_op jit(solution)/shard_map/ppermute | solution.py:35
  43.5 8.0 %collective-permute-start.3 = (bf16[256,256]{1,0:T(8,128)(2,1)S(1)}, bf16[256,256]{1,0:T(8,128)(2,1)S(1)}, u32[]{:S(2)}, u32[]{:S(2)}) collective-permute-start(bf16[256,256]{1,0:T(8,128)(2,1)S(1)} %get-tuple-element.12), channel_id=1, source_target_pairs={{0,192},{64,0},{128,64},{192,128},{1,193},{65,1},{129,65},{193,129... | collective-permute-start | bytes 393224 | tf_op jit(solution)/shard_map/ppermute | solution.py:39
  46.3 5.9 %collective-permute-start.2 = (bf16[256,256]{1,0:T(8,128)(2,1)S(1)}, bf16[256,256]{1,0:T(8,128)(2,1)S(1)}, u32[]{:S(2)}, u32[]{:S(2)}) collective-permute-start(bf16[256,256]{1,0:T(8,128)(2,1)S(1)} %get-tuple-element.13), channel_id=1, source_target_pairs={{0,128},{64,192},{128,0},{192,64},{1,129},{65,193},{129,1},{193,65... | collective-permute-start | bytes 393224 | tf_op jit(solution)/shard_map/ppermute | solution.py:39
  46.7 9.4 %collective-permute-start.1 = (bf16[256,256]{1,0:T(8,128)(2,1)S(1)}, bf16[256,256]{1,0:T(8,128)(2,1)S(1)}, u32[]{:S(2)}, u32[]{:S(2)}) collective-permute-start(bf16[256,256]{1,0:T(8,128)(2,1)S(1)} %get-tuple-element.11), channel_id=1, source_target_pairs={{0,64},{64,128},{128,192},{192,0},{1,65},{65,129},{129,193},{193,1... | collective-permute-start | bytes 393224 | tf_op jit(solution)/shard_map/ppermute | solution.py:39
  57.3 5.2 %collective-permute-start.9 = (bf16[80,256]{1,0:T(8,128)(2,1)S(1)}, bf16[80,256]{1,0:T(8,128)(2,1)S(1)}, u32[]{:S(2)}, u32[]{:S(2)}) collective-permute-start(bf16[80,256]{1,0:T(8,128)(2,1)S(1)} %get-tuple-element.33), channel_id=1, source_target_pairs={{0,192},{64,0},{128,64},{192,128},{1,193},{65,1},{129,65},{193,129... | collective-permute-start | bytes 122888 | tf_op jit(solution)/shard_map/ppermute | solution.py:39
  57.4 11.3 %collective-permute-start.6 = (bf16[256,256]{1,0:T(8,128)(2,1)S(1)}, bf16[256,256]{1,0:T(8,128)(2,1)S(1)}, u32[]{:S(2)}, u32[]{:S(2)}) collective-permute-start(bf16[256,256]{1,0:T(8,128)(2,1)S(1)} %get-tuple-element.39.refs_0_), channel_id=1, source_target_pairs={{0,192},{64,0},{128,64},{192,128},{1,193},{65,1},{129,65},{193,129... | collective-permute-start | bytes 393224 | tf_op jit(solution)/shard_map/ppermute | solution.py:39
  57.7 11.1 %collective-permute-start.7 = (bf16[256,256]{1,0:T(8,128)(2,1)S(1)}, bf16[256,256]{1,0:T(8,128)(2,1)S(1)}, u32[]{:S(2)}, u32[]{:S(2)}) collective-permute-start(bf16[256,256]{1,0:T(8,128)(2,1)S(1)} %get-tuple-element.39.refs_0_), channel_id=1, source_target_pairs={{0,128},{64,192},{128,0},{192,64},{1,129},{65,193},{129,1},{193,65... | collective-permute-start | bytes 393224 | tf_op jit(solution)/shard_map/ppermute | solution.py:39
  60.7 8.1 %collective-permute-start.8 = (bf16[256,256]{1,0:T(8,128)(2,1)S(1)}, bf16[256,256]{1,0:T(8,128)(2,1)S(1)}, u32[]{:S(2)}, u32[]{:S(2)}) collective-permute-start(bf16[256,256]{1,0:T(8,128)(2,1)S(1)} %get-tuple-element.39.refs_0_), channel_id=1, source_target_pairs={{0,64},{64,128},{128,192},{192,0},{1,65},{65,129},{129,193},{193,1... | collective-permute-start | bytes 393224 | tf_op jit(solution)/shard_map/ppermute | solution.py:39
  60.7 6.5 %collective-permute-start.10 = (bf16[80,256]{1,0:T(8,128)(2,1)S(1)}, bf16[80,256]{1,0:T(8,128)(2,1)S(1)}, u32[]{:S(2)}, u32[]{:S(2)}) collective-permute-start(bf16[80,256]{1,0:T(8,128)(2,1)S(1)} %get-tuple-element.34), channel_id=1, source_target_pairs={{0,128},{64,192},{128,0},{192,64},{1,129},{65,193},{129,1},{193,65... | collective-permute-start | bytes 122888 | tf_op jit(solution)/shard_map/ppermute | solution.py:39
  62.5 6.2 %collective-permute-start.11 = (bf16[80,256]{1,0:T(8,128)(2,1)S(1)}, bf16[80,256]{1,0:T(8,128)(2,1)S(1)}, u32[]{:S(2)}, u32[]{:S(2)}) collective-permute-start(bf16[80,256]{1,0:T(8,128)(2,1)S(1)} %get-tuple-element.32), channel_id=1, source_target_pairs={{0,64},{64,128},{128,192},{192,0},{1,65},{65,129},{129,193},{193,1... | collective-permute-start | bytes 122888 | tf_op jit(solution)/shard_map/ppermute | solution.py:39
  69.9 14.4 %all-to-all-start.1 = ((bf16[8,80,256]{2,1,0:T(8,128)(2,1)}), bf16[8,80,256]{2,1,0:T(8,128)(2,1)S(1)}, u32[]{:S(2)}, u32[]{:S(2)}) async-start(bf16[8,80,256]{2,1,0:T(8,128)(2,1)} %grad_parts.1), calls=%async_computation.1 | async-start | bytes 655360 | tf_op jit(solution)/shard_map/all_to_all | solution.py:27
  75.4 13.4 %collective-permute-start.4 = (f32[128,128]{1,0:T(8,128)S(1)}, f32[128,128]{1,0:T(8,128)S(1)}, u32[]{:S(2)}, u32[]{:S(2)}) collective-permute-start(f32[128,128]{1,0:T(8,128)S(1)} %slice_select_fusion), channel_id=1, source_target_pairs={{0,4},{4,0},{1,5},{5,1},{2,6},{6,2},{3,7},{7,3},{8,12},{12,8},{9,1... | collective-permute-start | bytes 196616 | tf_op jit(solution)/shard_map/ppermute | solution.py:35
  84.4 5.1 %collective-permute-start.13 = (f32[80,256]{1,0:T(8,128)S(1)}, f32[80,256]{1,0:T(8,128)S(1)}, u32[]{:S(2)}, u32[]{:S(2)}) collective-permute-start(f32[80,256]{1,0:T(8,128)S(1)} %convert_reduce_fusion), channel_id=1, source_target_pairs={{0,1},{1,2},{2,3},{3,0},{4,5},{5,6},{6,7},{7,4},{8,9},{9,10},{10,1... | collective-permute-start | bytes 245768 | tf_op jit(solution)/shard_map/ppermute | solution.py:39
  85.9 3.6 %collective-permute-start.14 = (f32[80,256]{1,0:T(8,128)S(1)}, f32[80,256]{1,0:T(8,128)S(1)}, u32[]{:S(2)}, u32[]{:S(2)}) collective-permute-start(f32[80,256]{1,0:T(8,128)S(1)} %convert_reduce_fusion), channel_id=1, source_target_pairs={{0,3},{1,0},{2,1},{3,2},{4,7},{5,4},{6,5},{7,6},{8,11},{9,8},{10,9... | collective-permute-start | bytes 245768 | tf_op jit(solution)/shard_map/ppermute | solution.py:39
  87.3 4.8 %collective-permute-start.12 = (f32[80,256]{1,0:T(8,128)S(1)}, f32[80,256]{1,0:T(8,128)S(1)}, u32[]{:S(2)}, u32[]{:S(2)}) collective-permute-start(f32[80,256]{1,0:T(8,128)S(1)} %convert_reduce_fusion), channel_id=1, source_target_pairs={{0,2},{1,3},{2,0},{3,1},{4,6},{5,7},{6,4},{7,5},{8,10},{9,11},{10,... | collective-permute-start | bytes 245768 | tf_op jit(solution)/shard_map/ppermute | solution.py:39
  92.9 14.0 %all-to-all-start.2 = ((f32[32,8,256]{2,1,0:T(8,128)}), f32[32,8,256]{2,1,0:T(8,128)S(1)}, u32[]{:S(2)}, u32[]{:S(2)}) async-start(f32[32,8,256]{2,1,0:T(8,128)} %broadcast_in_dim.5), calls=%async_computation.2 | async-start | bytes 524288 | tf_op jit(solution)/shard_map/all_to_all | solution.py:27
  97.3 5.3 %collective-permute-start.15 = (f32[40,256]{1,0:T(8,128)S(1)}, f32[40,256]{1,0:T(8,128)S(1)}, u32[]{:S(2)}, u32[]{:S(2)}) collective-permute-start(f32[40,256]{1,0:T(8,128)S(1)} %pad_maximum_fusion.9), channel_id=1, source_target_pairs={{0,4},{4,0},{1,5},{5,1},{2,6},{6,2},{3,7},{7,3},{8,12},{12,8},{9,1... | collective-permute-start | bytes 122888 | tf_op jit(solution)/shard_map/ppermute | solution.py:35
  106.9 6.8 %collective-permute-start.16 = (f32[256,256]{1,0:T(8,128)S(1)}, f32[256,256]{1,0:T(8,128)S(1)}, u32[]{:S(2)}, u32[]{:S(2)}) collective-permute-start(f32[256,256]{1,0:T(8,128)S(1)} %bitcast.53), channel_id=1, source_target_pairs={{0,4},{4,0},{1,5},{5,1},{2,6},{6,2},{3,7},{7,3},{8,12},{12,8},{9,1... | collective-permute-start | bytes 786440 | tf_op jit(solution)/shard_map/ppermute | solution.py:35

commit v4 on v3

--- a/solution.py
+++ b/solution.py
@@ -9,6 +9,7 @@
 
 Y, Z, CORES, REPS = 4, 8, 2, 4
 CHIPS = Y * Z
+LAST_TWICE = (2, 1, 3)
 SWAP = [(0, 1), (1, 0)]
 
 
@@ -44,8 +45,10 @@
 
 
 def rep_sum(value):
-    terms = [value] + [shift(value, "rep", REPS, by) for by in range(1, REPS)]
-    return paired(terms)
+    terms = {0: value}
+    for by in LAST_TWICE:
+        terms[by] = shift(value, "rep", REPS, by)
+    return (terms[1] + terms[3]) + (terms[0] + terms[2])
 
 
 def gather_kernel(neighbours, owners, feats, edges, own, near, out, *, per_step):
@@ -92,7 +95,7 @@
     blocks, fan, rows, _ = edges.shape
     width = feats.shape[0]
     columns = Y * CORES * rows + own.shape[1]
-    per_step = 8
+    per_step = 16
     return pl.pallas_call(
         functools.partial(gather_kernel, per_step=per_step),
         out_shape=jax.ShapeDtypeStruct((Z, 2 * width, columns), feats.dtype),
@@ -122,6 +125,7 @@
     half = out.shape[2]
     rows = mine.shape[0] // Z
     layer_rows = mine.shape[1] - 2 * half
+    pieces = (pieces[0], pieces[2], pieces[1], pieces[3])
     d_all = jnp.concatenate([piece[...] for piece in pieces], 0)
     for i, feats in enumerate((mine[:, half : half + layer_rows], other[:, :layer_rows])):
         grads = jnp.dot(feats, d_all, preferred_element_type=jnp.float32).astype(out.dtype)
@@ -218,7 +222,7 @@
     partial = dot(feats_mine, weights_mine, 0, 0) + dot(feats_other, weights_other, 0, 0)
     partial = partial.astype(jnp.bfloat16).reshape(Y, span, half)
     pre = partial[0].astype(jnp.float32)
-    for by in range(1, Y):
+    for by in LAST_TWICE:
         pre = pre + shift(partial[by], "y", Y, by).astype(jnp.float32)
     pre = pre + columns(bias_one, core)
 
@@ -246,7 +250,7 @@
     bias = jnp.pad(bias, ((0, pad - CORES), (0, 0)))
     per_y = half // Y
     pieces, extras = [d_pre], []
-    for by in range(1, Y):
+    for by in LAST_TWICE:
         pieces.append(shift(d_pre, "y", Y, -by))
     for by in range(Y):
         piece = lax.dynamic_slice_in_dim(heads, ((at_y - by) % Y) * per_y, per_y, 0)

time: 115 us -> 112 us (0.974)
  waiting for transfers between devices: 47.9 us -> 41.6 us
  starting transfers between devices: 45.2 us -> 49.5 us
    ppermute x12, waiting for transfers between devices: 14.1 us -> 10.1 us  [shift(): lax.ppermute(value, axis, [(i, (i + by) % count) for i in range(count)])]
    all_to_all x3, waiting for transfers between devices: 32.5 us -> 30.1 us  [exchange(): return lax.all_to_all(value, axes, 0, 0, tiled=True)]
    ppermute x12, starting transfers between devices: 14.9 us -> 17.2 us  [shift(): lax.ppermute(value, axis, [(i, (i + by) % count) for i in range(count)])]
    ppermute x5, starting transfers between devices: 13.5 us -> 15.2 us  [swap(): return lax.ppermute(value, 'core', SWAP)]
  transfers between devices with their start and end apart: 20 -> 20, of which waited for: 11 -> 10; matrix products, arithmetic and copies ran while one was open for 6% -> 7% of each run, Pallas kernels for 0% -> 0%
where the time goes in v4:
time: 112 us
  starting transfers between devices  49.5 us (44%)
  waiting for transfers between devices  41.6 us (37%)
  Pallas kernels  7.97 us (7%)
  matrix products  4.99 us (4%)
  other arithmetic  3.41 us (3%)
  between operations  2.26 us (2%)
  local copies, waits for them, and re-layouts  2.2 us (2%)
    all_to_all x3, waiting for transfers between devices, exchange(): return lax.all_to_all(value, axes, 0, 0, tiled=True)  30.1 us
    ppermute x12, starting transfers between devices, shift(): lax.ppermute(value, axis, [(i, (i + by) % count) for i in range(count)])  17.2 us
    all_to_all x3, starting transfers between devices, exchange(): return lax.all_to_all(value, axes, 0, 0, tiled=True)  17.1 us
    ppermute x5, starting transfers between devices, swap(): return lax.ppermute(value, 'core', SWAP)  15.2 us
    ppermute x12, waiting for transfers between devices, shift(): lax.ppermute(value, axis, [(i, (i + by) % count) for i in range(count)])  10.1 us
    pallas_call x1, Pallas kernels, gather_rows(): pl.pallas_call(functools.partial(gather_kernel, per_step=per_step), out_s...  6.81 us
    dot_general x12, matrix products, dot(): lax.dot_general(left, right, (((left_dim,), (right_dim,)), ((), ())), pre...  4.31 us
  transfers between devices with their start and end apart: 20, of which 10 were waited for; matrix products, arithmetic and copies ran while one was open for 7% of the time, Pallas kernels for 0%

profile of v4, /device:TPU:1, one launch (start us, length us, event | category | flops | bytes accessed | tf_op | source)
XLA Modules:
  0.0 111.9 jit_solution(825037966751276503)
XLA Ops:
  0.7 6.8 %gather_rows.1 = bf16[8,32,1536]{2,1,0:T(8,128)(2,1)} custom-call(s32[8,32]{1,0:T(8,128)} %bitcast.55, s32[1,32]{1,0:T(1,128)} %owners.1, bf16[16,32768]{1,0:T(8,128)(2,1)} %feats.1, bf16[32,8,128,128]{3,2,1,0:T(8,128)(2,1)} %bitcast.52, bf16[16,512]{1,0:T(8,128)(2,1)} %own.1, bf16[16,512]{1,0:T(8,128)(2,1)} %near.1), custom_call_target="tpu_custom_call" | custom-call | flops 134217728 | bytes 9437184 | tf_op jit(solution)/shard_map/gather_rows/pallas_call | solution.py:99
  7.5 9.0 %all-to-all-start = ((bf16[8,32,1536]{2,1,0:T(8,128)(2,1)}), bf16[8,32,1536]{2,1,0:T(8,128)(2,1)S(1)}, u32[]{:S(2)}, u32[]{:S(2)}) async-start(bf16[8,32,1536]{2,1,0:T(8,128)(2,1)} %gather_rows.1), calls=%async_computation | async-start | bytes 1572864 | tf_op jit(solution)/shard_map/all_to_all | solution.py:28
  16.5 1.0 collective-permute-start.5
  17.6 0.2 compare_reduce_fusion
  17.8 0.7 convolution_convert_fusion.3
  19.0 21.1 %all-to-all-done = bf16[8,32,1536]{2,1,0:T(8,128)(2,1)S(1)} async-done(((bf16[8,32,1536]{2,1,0:T(8,128)(2,1)}), bf16[8,32,1536]{2,1,0:T(8,128)(2,1)S(1)}, u32[]{:S(2)}, u32[]{:S(2)}) %all-to-all-start) | async-done | bytes 786464 | tf_op jit(solution)/shard_map/all_to_all | solution.py:28
  40.1 0.6 collective-permute-start
  40.7 0.2 convolution_convert_fusion
  40.9 0.2 fusion.10
  41.1 0.4 fusion.5
  41.5 1.0 collective-permute-done.refs_9_
  42.5 0.4 fusion
  42.8 2.8 %collective-permute-start.3 = (bf16[256,256]{1,0:T(8,128)(2,1)S(1)}, bf16[256,256]{1,0:T(8,128)(2,1)S(1)}, u32[]{:S(2)}, u32[]{:S(2)}) collective-permute-start(bf16[256,256]{1,0:T(8,128)(2,1)S(1)} %get-tuple-element.12), channel_id=1, source_target_pairs={{0,192},{64,0},{128,64},{192,128},{1,193},{65,1},{129,65},{193,129... | collective-permute-start | bytes 393224 | tf_op jit(solution)/shard_map/ppermute | solution.py:40
  45.7 1.6 %collective-permute-start.1 = (bf16[256,256]{1,0:T(8,128)(2,1)S(1)}, bf16[256,256]{1,0:T(8,128)(2,1)S(1)}, u32[]{:S(2)}, u32[]{:S(2)}) collective-permute-start(bf16[256,256]{1,0:T(8,128)(2,1)S(1)} %get-tuple-element.11), channel_id=1, source_target_pairs={{0,128},{64,192},{128,0},{192,64},{1,129},{65,193},{129,1},{193,65... | collective-permute-start | bytes 393224 | tf_op jit(solution)/shard_map/ppermute | solution.py:40
  47.3 0.2 fusion.12
  47.5 0.7 collective-permute-done.3
  48.2 6.1 %collective-permute-done.2 = bf16[256,256]{1,0:T(8,128)(2,1)S(1)} collective-permute-done((bf16[256,256]{1,0:T(8,128)(2,1)S(1)}, bf16[256,256]{1,0:T(8,128)(2,1)S(1)}, u32[]{:S(2)}, u32[]{:S(2)}) %collective-permute-start.2) | collective-permute-done | bytes 131104 | tf_op jit(solution)/shard_map/ppermute | solution.py:40
  54.7 0.2 convolution_convert_fusion.5
  55.0 0.3 fusion.50
  55.3 0.2 convolution_convert_fusion.4
  55.7 0.5 collective-permute-start.6
  56.1 3.4 %collective-permute-start.7 = (bf16[256,256]{1,0:T(8,128)(2,1)S(1)}, bf16[256,256]{1,0:T(8,128)(2,1)S(1)}, u32[]{:S(2)}, u32[]{:S(2)}) collective-permute-start(bf16[256,256]{1,0:T(8,128)(2,1)S(1)} %get-tuple-element.39.refs_0_), channel_id=1, source_target_pairs={{0,192},{64,0},{128,64},{192,128},{1,193},{65,1},{129,65},{193,129... | collective-permute-start | bytes 393224 | tf_op jit(solution)/shard_map/ppermute | solution.py:40
  59.5 1.2 %collective-permute-start.10 = (bf16[80,256]{1,0:T(8,128)(2,1)S(1)}, bf16[80,256]{1,0:T(8,128)(2,1)S(1)}, u32[]{:S(2)}, u32[]{:S(2)}) collective-permute-start(bf16[80,256]{1,0:T(8,128)(2,1)S(1)} %get-tuple-element.34), channel_id=1, source_target_pairs={{0,128},{64,192},{128,0},{192,64},{1,129},{65,193},{129,1},{193,65... | collective-permute-start | bytes 122888 | tf_op jit(solution)/shard_map/ppermute | solution.py:40
  60.7 2.1 %collective-permute-start.11 = (bf16[80,256]{1,0:T(8,128)(2,1)S(1)}, bf16[80,256]{1,0:T(8,128)(2,1)S(1)}, u32[]{:S(2)}, u32[]{:S(2)}) collective-permute-start(bf16[80,256]{1,0:T(8,128)(2,1)S(1)} %get-tuple-element.32), channel_id=1, source_target_pairs={{0,64},{64,128},{128,192},{192,0},{1,65},{65,129},{129,193},{193,1... | collective-permute-start | bytes 122888 | tf_op jit(solution)/shard_map/ppermute | solution.py:40
  62.8 0.6 fusion.49
  64.7 0.5 collective-permute-done.10.refs_6_
  65.2 1.6 %collective-permute-done.11.refs_7_ = bf16[80,256]{1,0:T(8,128)(2,1)S(1)} collective-permute-done((bf16[80,256]{1,0:T(8,128)(2,1)S(1)}, bf16[80,256]{1,0:T(8,128)(2,1)S(1)}, u32[]{:S(2)}, u32[]{:S(2)}) %collective-permute-start.11) | collective-permute-done | bytes 40992 | tf_op jit(solution)/shard_map/ppermute | solution.py:40
  66.8 1.2 %grad_parts.1 = bf16[8,80,256]{2,1,0:T(8,128)(2,1)} custom-call(bf16[256,256]{1,0:T(8,128)(2,1)S(1)} %get-tuple-element.39.refs_0_, bf16[256,256]{1,0:T(8,128)(2,1)S(1)} %collective-permute-done.6.refs_1_, bf16[256,256]{1,0:T(8,128)(2,1)S(1)} %collective-permute-done.7.refs_2_, bf16[256,256]{1,0:T(8,128)(2,1)S(1)} %collective-permute-done.8.refs_3_, ...), custom_call_target="tpu_custom_call" | custom-call | flops 268435456 | bytes 1966080 | tf_op jit(solution)/shard_map/grad_parts/pallas_call | solution.py:145
  67.9 3.4 %all-to-all-start.1 = ((bf16[8,80,256]{2,1,0:T(8,128)(2,1)}), bf16[8,80,256]{2,1,0:T(8,128)(2,1)S(1)}, u32[]{:S(2)}, u32[]{:S(2)}) async-start(bf16[8,80,256]{2,1,0:T(8,128)(2,1)} %grad_parts.1), calls=%async_computation.1 | async-start | bytes 655360 | tf_op jit(solution)/shard_map/all_to_all | solution.py:28
  71.4 1.0 fusion.19
  72.4 1.0 convolution_add_fusion.2
  73.4 2.6 %collective-permute-start.4 = (f32[128,128]{1,0:T(8,128)S(1)}, f32[128,128]{1,0:T(8,128)S(1)}, u32[]{:S(2)}, u32[]{:S(2)}) collective-permute-start(f32[128,128]{1,0:T(8,128)S(1)} %slice_select_fusion), channel_id=1, source_target_pairs={{0,4},{4,0},{1,5},{5,1},{2,6},{6,2},{3,7},{7,3},{8,12},{12,8},{9,1... | collective-permute-start | bytes 196616 | tf_op jit(solution)/shard_map/ppermute | solution.py:36
  76.1 5.2 %all-to-all-done.1 = bf16[8,80,256]{2,1,0:T(8,128)(2,1)S(1)} async-done(((bf16[8,80,256]{2,1,0:T(8,128)(2,1)}), bf16[8,80,256]{2,1,0:T(8,128)(2,1)S(1)}, u32[]{:S(2)}, u32[]{:S(2)}) %all-to-all-start.1) | async-done | bytes 327712 | tf_op jit(solution)/shard_map/all_to_all | solution.py:28
  81.3 2.8 %collective-permute-start.14 = (f32[80,256]{1,0:T(8,128)S(1)}, f32[80,256]{1,0:T(8,128)S(1)}, u32[]{:S(2)}, u32[]{:S(2)}) collective-permute-start(f32[80,256]{1,0:T(8,128)S(1)} %convert_reduce_fusion), channel_id=1, source_target_pairs={{0,2},{1,3},{2,0},{3,1},{4,6},{5,7},{6,4},{7,5},{8,10},{9,11},{10,... | collective-permute-start | bytes 245768 | tf_op jit(solution)/shard_map/ppermute | solution.py:40
  84.2 0.3 collective-permute-start.12
  84.5 2.4 %collective-permute-start.13 = (f32[80,256]{1,0:T(8,128)S(1)}, f32[80,256]{1,0:T(8,128)S(1)}, u32[]{:S(2)}, u32[]{:S(2)}) collective-permute-start(f32[80,256]{1,0:T(8,128)S(1)} %convert_reduce_fusion), channel_id=1, source_target_pairs={{0,3},{1,0},{2,1},{3,2},{4,7},{5,4},{6,5},{7,6},{8,11},{9,8},{10,9... | collective-permute-start | bytes 245768 | tf_op jit(solution)/shard_map/ppermute | solution.py:40
  86.9 0.6 fusion.21
  87.5 1.2 %collective-permute-done.12 = f32[80,256]{1,0:T(8,128)S(1)} collective-permute-done((f32[80,256]{1,0:T(8,128)S(1)}, f32[80,256]{1,0:T(8,128)S(1)}, u32[]{:S(2)}, u32[]{:S(2)}) %collective-permute-start.12) | collective-permute-done | bytes 81952 | tf_op jit(solution)/shard_map/ppermute | solution.py:40
  88.7 0.7 broadcast_in_dim.5
  89.5 4.7 %all-to-all-start.2 = ((f32[32,8,256]{2,1,0:T(8,128)}), f32[32,8,256]{2,1,0:T(8,128)S(1)}, u32[]{:S(2)}, u32[]{:S(2)}) async-start(f32[32,8,256]{2,1,0:T(8,128)} %broadcast_in_dim.5), calls=%async_computation.2 | async-start | bytes 524288 | tf_op jit(solution)/shard_map/all_to_all | solution.py:28
  94.1 5.0 %collective-permute-start.15 = (f32[40,256]{1,0:T(8,128)S(1)}, f32[40,256]{1,0:T(8,128)S(1)}, u32[]{:S(2)}, u32[]{:S(2)}) collective-permute-start(f32[40,256]{1,0:T(8,128)S(1)} %pad_maximum_fusion.9), channel_id=1, source_target_pairs={{0,4},{4,0},{1,5},{5,1},{2,6},{6,2},{3,7},{7,3},{8,12},{12,8},{9,1... | collective-permute-start | bytes 122888 | tf_op jit(solution)/shard_map/ppermute | solution.py:36
  99.1 0.5 slice_bitcast_fusion
  99.6 0.4 collective-permute-done.15
  100.0 3.8 %all-to-all-done.2 = f32[32,8,256]{2,1,0:T(8,128)S(1)} async-done(((f32[32,8,256]{2,1,0:T(8,128)}), f32[32,8,256]{2,1,0:T(8,128)S(1)}, u32[]{:S(2)}, u32[]{:S(2)}) %all-to-all-start.2) | async-done | bytes 262176 | tf_op jit(solution)/shard_map/all_to_all | solution.py:28
  103.8 6.0 %collective-permute-start.16 = (f32[256,256]{1,0:T(8,128)S(1)}, f32[256,256]{1,0:T(8,128)S(1)}, u32[]{:S(2)}, u32[]{:S(2)}) collective-permute-start(f32[256,256]{1,0:T(8,128)S(1)} %bitcast.53), channel_id=1, source_target_pairs={{0,4},{4,0},{1,5},{5,1},{2,6},{6,2},{3,7},{7,3},{8,12},{12,8},{9,1... | collective-permute-start | bytes 786440 | tf_op jit(solution)/shard_map/ppermute | solution.py:36
  109.8 0.6 pad_maximum_fusion.11
  110.4 0.6 pad_maximum_fusion.10
  111.1 0.8 pad_maximum_fusion
  (55 shorter events, 1.3 us)
Async XLA Ops:
  0.6 17.1 %copy-start = (bf16[1,32,128,128]{3,2,1,0:T(8,128)(2,1)S(1)}, bf16[1,32,128,128]{3,2,1,0:T(8,128)(2,1)}, u32[]{:S(2)}) copy-start(bf16[1,32,128,128]{3,2,1,0:T(8,128)(2,1)} %param.15) | copy-start | bytes 3145732
  0.7 16.9 %copy-start.4 = (s32[1,32]{1,0:T(1,128)S(1)}, s32[1,32]{1,0:T(1,128)}, u32[]{:S(2)}) copy-start(s32[1,32]{1,0:T(1,128)} %owners.1) | copy-start | bytes 388
  0.7 15.9 %copy-start.3 = (bf16[1,128,128]{2,1,0:T(8,128)(2,1)S(1)}, bf16[1,128,128]{2,1,0:T(8,128)(2,1)}, u32[]{:S(2)}) copy-start(bf16[1,128,128]{2,1,0:T(8,128)(2,1)} %param.23) | copy-start | bytes 98308
  0.7 18.0 %copy-start.6 = (f32[512]{0:T(512)S(1)}, f32[512]{0:T(512)}, u32[]{:S(2)}) copy-start(f32[512]{0:T(512)} %param.19) | copy-start | bytes 6148
  0.7 40.1 %copy-start.1 = (bf16[512,128]{1,0:T(8,128)(2,1)S(1)}, bf16[512,128]{1,0:T(8,128)(2,1)}, u32[]{:S(2)}) copy-start(bf16[512,128]{1,0:T(8,128)(2,1)} %param.21) | copy-start | bytes 393220
  0.7 54.3 %copy-start.2 = (bf16[512,128]{1,0:T(8,128)(2,1)S(1)}, bf16[512,128]{1,0:T(8,128)(2,1)}, u32[]{:S(2)}) copy-start(bf16[512,128]{1,0:T(8,128)(2,1)} %param.20) | copy-start | bytes 393220
  7.5 32.6 %all-to-all-start = ((bf16[8,32,1536]{2,1,0:T(8,128)(2,1)}), bf16[8,32,1536]{2,1,0:T(8,128)(2,1)S(1)}, u32[]{:S(2)}, u32[]{:S(2)}) async-start(bf16[8,32,1536]{2,1,0:T(8,128)(2,1)} %gather_rows.1), calls=%async_computation | async-start | bytes 1572864 | tf_op jit(solution)/shard_map/all_to_all | solution.py:28
  16.5 2.2 %collective-permute-start.5 = (bf16[128,128]{1,0:T(8,128)(2,1)S(1)}, bf16[128,128]{1,0:T(8,128)(2,1)S(1)}, u32[]{:S(2)}, u32[]{:S(2)}) collective-permute-start(bf16[128,128]{1,0:T(8,128)(2,1)S(1)} %bitcast.54), channel_id=1, source_target_pairs={{0,4},{4,0},{1,5},{5,1},{2,6},{6,2},{3,7},{7,3},{8,12},{12,8},{9,1... | collective-permute-start | bytes 98312 | tf_op jit(solution)/shard_map/ppermute | solution.py:36
  18.5 68.4 %copy-start.5 = (f32[128]{0:T(128)S(1)}, f32[128]{0:T(128)}, u32[]{:S(2)}) copy-start(f32[128]{0:T(128)} %param.22) | copy-start | bytes 1540
  40.1 2.3 %collective-permute-start = (bf16[256,1280]{1,0:T(8,128)(2,1)S(1)}, bf16[256,1280]{1,0:T(8,128)(2,1)S(1)}, u32[]{:S(2)}, u32[]{:S(2)}) collective-permute-start(bf16[256,1280]{1,0:T(8,128)(2,1)S(1)} %slice.138), channel_id=1, source_target_pairs={{0,4},{4,0},{1,5},{5,1},{2,6},{6,2},{3,7},{7,3},{8,12},{12,8},{9,1... | collective-permute-start | bytes 1966088 | tf_op jit(solution)/shard_map/ppermute | solution.py:36
  42.8 5.3 %collective-permute-start.3 = (bf16[256,256]{1,0:T(8,128)(2,1)S(1)}, bf16[256,256]{1,0:T(8,128)(2,1)S(1)}, u32[]{:S(2)}, u32[]{:S(2)}) collective-permute-start(bf16[256,256]{1,0:T(8,128)(2,1)S(1)} %get-tuple-element.12), channel_id=1, source_target_pairs={{0,192},{64,0},{128,64},{192,128},{1,193},{65,1},{129,65},{193,129... | collective-permute-start | bytes 393224 | tf_op jit(solution)/shard_map/ppermute | solution.py:40
  45.7 8.6 %collective-permute-start.2 = (bf16[256,256]{1,0:T(8,128)(2,1)S(1)}, bf16[256,256]{1,0:T(8,128)(2,1)S(1)}, u32[]{:S(2)}, u32[]{:S(2)}) collective-permute-start(bf16[256,256]{1,0:T(8,128)(2,1)S(1)} %get-tuple-element.13), channel_id=1, source_target_pairs={{0,64},{64,128},{128,192},{192,0},{1,65},{65,129},{129,193},{193,1... | collective-permute-start | bytes 393224 | tf_op jit(solution)/shard_map/ppermute | solution.py:40
  45.7 8.6 %collective-permute-start.1 = (bf16[256,256]{1,0:T(8,128)(2,1)S(1)}, bf16[256,256]{1,0:T(8,128)(2,1)S(1)}, u32[]{:S(2)}, u32[]{:S(2)}) collective-permute-start(bf16[256,256]{1,0:T(8,128)(2,1)S(1)} %get-tuple-element.11), channel_id=1, source_target_pairs={{0,128},{64,192},{128,0},{192,64},{1,129},{65,193},{129,1},{193,65... | collective-permute-start | bytes 393224 | tf_op jit(solution)/shard_map/ppermute | solution.py:40
  55.6 5.1 %collective-permute-start.9 = (bf16[80,256]{1,0:T(8,128)(2,1)S(1)}, bf16[80,256]{1,0:T(8,128)(2,1)S(1)}, u32[]{:S(2)}, u32[]{:S(2)}) collective-permute-start(bf16[80,256]{1,0:T(8,128)(2,1)S(1)} %get-tuple-element.33), channel_id=1, source_target_pairs={{0,192},{64,0},{128,64},{192,128},{1,193},{65,1},{129,65},{193,129... | collective-permute-start | bytes 122888 | tf_op jit(solution)/shard_map/ppermute | solution.py:40
  55.7 11.1 %collective-permute-start.6 = (bf16[256,256]{1,0:T(8,128)(2,1)S(1)}, bf16[256,256]{1,0:T(8,128)(2,1)S(1)}, u32[]{:S(2)}, u32[]{:S(2)}) collective-permute-start(bf16[256,256]{1,0:T(8,128)(2,1)S(1)} %get-tuple-element.39.refs_0_), channel_id=1, source_target_pairs={{0,128},{64,192},{128,0},{192,64},{1,129},{65,193},{129,1},{193,65... | collective-permute-start | bytes 393224 | tf_op jit(solution)/shard_map/ppermute | solution.py:40
  56.1 10.6 %collective-permute-start.7 = (bf16[256,256]{1,0:T(8,128)(2,1)S(1)}, bf16[256,256]{1,0:T(8,128)(2,1)S(1)}, u32[]{:S(2)}, u32[]{:S(2)}) collective-permute-start(bf16[256,256]{1,0:T(8,128)(2,1)S(1)} %get-tuple-element.39.refs_0_), channel_id=1, source_target_pairs={{0,192},{64,0},{128,64},{192,128},{1,193},{65,1},{129,65},{193,129... | collective-permute-start | bytes 393224 | tf_op jit(solution)/shard_map/ppermute | solution.py:40
  59.5 7.3 %collective-permute-start.8 = (bf16[256,256]{1,0:T(8,128)(2,1)S(1)}, bf16[256,256]{1,0:T(8,128)(2,1)S(1)}, u32[]{:S(2)}, u32[]{:S(2)}) collective-permute-start(bf16[256,256]{1,0:T(8,128)(2,1)S(1)} %get-tuple-element.39.refs_0_), channel_id=1, source_target_pairs={{0,64},{64,128},{128,192},{192,0},{1,65},{65,129},{129,193},{193,1... | collective-permute-start | bytes 393224 | tf_op jit(solution)/shard_map/ppermute | solution.py:40
  59.5 5.7 %collective-permute-start.10 = (bf16[80,256]{1,0:T(8,128)(2,1)S(1)}, bf16[80,256]{1,0:T(8,128)(2,1)S(1)}, u32[]{:S(2)}, u32[]{:S(2)}) collective-permute-start(bf16[80,256]{1,0:T(8,128)(2,1)S(1)} %get-tuple-element.34), channel_id=1, source_target_pairs={{0,128},{64,192},{128,0},{192,64},{1,129},{65,193},{129,1},{193,65... | collective-permute-start | bytes 122888 | tf_op jit(solution)/shard_map/ppermute | solution.py:40
  60.7 6.1 %collective-permute-start.11 = (bf16[80,256]{1,0:T(8,128)(2,1)S(1)}, bf16[80,256]{1,0:T(8,128)(2,1)S(1)}, u32[]{:S(2)}, u32[]{:S(2)}) collective-permute-start(bf16[80,256]{1,0:T(8,128)(2,1)S(1)} %get-tuple-element.32), channel_id=1, source_target_pairs={{0,64},{64,128},{128,192},{192,0},{1,65},{65,129},{129,193},{193,1... | collective-permute-start | bytes 122888 | tf_op jit(solution)/shard_map/ppermute | solution.py:40
  67.9 13.3 %all-to-all-start.1 = ((bf16[8,80,256]{2,1,0:T(8,128)(2,1)}), bf16[8,80,256]{2,1,0:T(8,128)(2,1)S(1)}, u32[]{:S(2)}, u32[]{:S(2)}) async-start(bf16[8,80,256]{2,1,0:T(8,128)(2,1)} %grad_parts.1), calls=%async_computation.1 | async-start | bytes 655360 | tf_op jit(solution)/shard_map/all_to_all | solution.py:28
  73.4 13.4 %collective-permute-start.4 = (f32[128,128]{1,0:T(8,128)S(1)}, f32[128,128]{1,0:T(8,128)S(1)}, u32[]{:S(2)}, u32[]{:S(2)}) collective-permute-start(f32[128,128]{1,0:T(8,128)S(1)} %slice_select_fusion), channel_id=1, source_target_pairs={{0,4},{4,0},{1,5},{5,1},{2,6},{6,2},{3,7},{7,3},{8,12},{12,8},{9,1... | collective-permute-start | bytes 196616 | tf_op jit(solution)/shard_map/ppermute | solution.py:36
  81.3 6.2 %collective-permute-start.14 = (f32[80,256]{1,0:T(8,128)S(1)}, f32[80,256]{1,0:T(8,128)S(1)}, u32[]{:S(2)}, u32[]{:S(2)}) collective-permute-start(f32[80,256]{1,0:T(8,128)S(1)} %convert_reduce_fusion), channel_id=1, source_target_pairs={{0,2},{1,3},{2,0},{3,1},{4,6},{5,7},{6,4},{7,5},{8,10},{9,11},{10,... | collective-permute-start | bytes 245768 | tf_op jit(solution)/shard_map/ppermute | solution.py:40
  84.2 4.5 %collective-permute-start.12 = (f32[80,256]{1,0:T(8,128)S(1)}, f32[80,256]{1,0:T(8,128)S(1)}, u32[]{:S(2)}, u32[]{:S(2)}) collective-permute-start(f32[80,256]{1,0:T(8,128)S(1)} %convert_reduce_fusion), channel_id=1, source_target_pairs={{0,1},{1,2},{2,3},{3,0},{4,5},{5,6},{6,7},{7,4},{8,9},{9,10},{10,1... | collective-permute-start | bytes 245768 | tf_op jit(solution)/shard_map/ppermute | solution.py:40
  84.5 4.2 %collective-permute-start.13 = (f32[80,256]{1,0:T(8,128)S(1)}, f32[80,256]{1,0:T(8,128)S(1)}, u32[]{:S(2)}, u32[]{:S(2)}) collective-permute-start(f32[80,256]{1,0:T(8,128)S(1)} %convert_reduce_fusion), channel_id=1, source_target_pairs={{0,3},{1,0},{2,1},{3,2},{4,7},{5,4},{6,5},{7,6},{8,11},{9,8},{10,9... | collective-permute-start | bytes 245768 | tf_op jit(solution)/shard_map/ppermute | solution.py:40
  89.5 14.3 %all-to-all-start.2 = ((f32[32,8,256]{2,1,0:T(8,128)}), f32[32,8,256]{2,1,0:T(8,128)S(1)}, u32[]{:S(2)}, u32[]{:S(2)}) async-start(f32[32,8,256]{2,1,0:T(8,128)} %broadcast_in_dim.5), calls=%async_computation.2 | async-start | bytes 524288 | tf_op jit(solution)/shard_map/all_to_all | solution.py:28
  94.1 5.8 %collective-permute-start.15 = (f32[40,256]{1,0:T(8,128)S(1)}, f32[40,256]{1,0:T(8,128)S(1)}, u32[]{:S(2)}, u32[]{:S(2)}) collective-permute-start(f32[40,256]{1,0:T(8,128)S(1)} %pad_maximum_fusion.9), channel_id=1, source_target_pairs={{0,4},{4,0},{1,5},{5,1},{2,6},{6,2},{3,7},{7,3},{8,12},{12,8},{9,1... | collective-permute-start | bytes 122888 | tf_op jit(solution)/shard_map/ppermute | solution.py:36
  103.8 7.2 %collective-permute-start.16 = (f32[256,256]{1,0:T(8,128)S(1)}, f32[256,256]{1,0:T(8,128)S(1)}, u32[]{:S(2)}, u32[]{:S(2)}) collective-permute-start(f32[256,256]{1,0:T(8,128)S(1)} %bitcast.53), channel_id=1, source_target_pairs={{0,4},{4,0},{1,5},{5,1},{2,6},{6,2},{3,7},{7,3},{8,12},{12,8},{9,1... | collective-permute-start | bytes 786440 | tf_op jit(solution)/shard_map/ppermute | solution.py:36

commit v5 on v4

--- a/solution.py
+++ b/solution.py
@@ -121,7 +121,7 @@
 
 
 def grads_kernel(*refs):
-    pieces, extras, (mine, other, out) = refs[:Y], refs[Y : 2 * Y], refs[2 * Y :]
+    pieces, extras, (bias, mine, other, out) = refs[:Y], refs[Y : 2 * Y], refs[2 * Y :]
     half = out.shape[2]
     rows = mine.shape[0] // Z
     layer_rows = mine.shape[1] - 2 * half
@@ -133,13 +133,15 @@
             out[z, i * rows : (i + 1) * rows] = grads[z * rows : (z + 1) * rows]
     extra = paired([piece[...].astype(jnp.float32) for piece in extras])
     per = half // CHIPS
-    bias = extra[Z * per : Z * per + 8]
+    first_row = lax.broadcasted_iota(jnp.int32, bias.shape, 0) == 0
+    sums = paired([jnp.sum(piece[...].astype(jnp.float32), 0, keepdims=True) for piece in pieces])
+    sums = jnp.where(first_row, sums, bias[...])
     for z in range(Z):
-        block = jnp.concatenate([extra[z * per : (z + 1) * per], bias], 0)
+        block = jnp.concatenate([extra[z * per : (z + 1) * per], sums], 0)
         out[z, CORES * rows :] = block.astype(out.dtype)
 
 
-def grad_parts(pieces, extras, mine, other):
+def grad_parts(pieces, extras, bias, mine, other):
     half = pieces[0].shape[1]
     rows = CORES * mine.shape[0] // Z + half // CHIPS + 8
     return pl.pallas_call(
@@ -152,7 +154,7 @@
             transcendentals=0,
         ),
         name="grad_parts",
-    )(*pieces, *extras, mine, other)
+    )(*pieces, *extras, bias, mine, other)
 
 
 def on_device(
@@ -212,6 +214,9 @@
     )
     upstream = upstream * filled.astype(jnp.bfloat16)[:, None, None]
     up_rows = upstream.reshape(span, out)
+    bias = jnp.sum(up_rows.astype(jnp.float32), 0)
+    bias = jnp.pad(bias[None], ((1, 6), (0, half - out)))
+    bias = paired([bias] + [shift(bias, "y", Y, -by) for by in range(1, Y)])
     self_half = lax.dynamic_slice_in_dim(self_out, core * half, half, 0)
     neigh_half = lax.dynamic_slice_in_dim(neigh_out, core * half, half, 0)
     d_mixed = dot(up_rows, neigh_half, 1, 1).astype(jnp.bfloat16).reshape(CORES, rows, half)
@@ -240,24 +245,15 @@
 
     heads = jnp.concatenate([dot(hidden, up_rows, 0, 0), dot(mixed, up_rows, 0, 0)], 1)
     heads = heads.astype(jnp.bfloat16)
-    bias = jnp.stack(
-        [
-            jnp.sum(d_pre.astype(jnp.float32), 0),
-            jnp.pad(jnp.sum(up_rows.astype(jnp.float32), 0), (0, half - out)),
-        ]
-    ).astype(jnp.bfloat16)
-    pad = 16
-    bias = jnp.pad(bias, ((0, pad - CORES), (0, 0)))
     per_y = half // Y
     pieces, extras = [d_pre], []
     for by in LAST_TWICE:
         pieces.append(shift(d_pre, "y", Y, -by))
     for by in range(Y):
         piece = lax.dynamic_slice_in_dim(heads, ((at_y - by) % Y) * per_y, per_y, 0)
-        piece = jnp.concatenate([piece, bias], 0)
         extras.append(piece if by == 0 else shift(piece, "y", Y, -by))
     per_z = per_y // Z
-    sums = exchange(grad_parts(pieces, extras, arrived, from_other), "z")
+    sums = exchange(grad_parts(pieces, extras, bias, arrived, from_other), "z")
     sums = jnp.sum(sums.astype(jnp.float32), 0)
     sums = rep_sum(sums)
     grads_mine, grads_other = sums[: 2 * width], sums[2 * width : 4 * width]

time: 112 us -> 112 us (level)
  starting transfers between devices: 49.5 us -> 55.8 us
  waiting for transfers between devices: 41.6 us -> 36.3 us
  matrix products: 4.99 us -> 3.28 us
    ppermute x12 -> x15, starting transfers between devices: 17.2 us -> 22.4 us  [shift(): lax.ppermute(value, axis, [(i, (i + by) % count) for i in range(count)])]
    all_to_all x3, waiting for transfers between devices: 30.1 us -> 26.2 us  [exchange(): return lax.all_to_all(value, axes, 0, 0, tiled=True)]
    ppermute x5, starting transfers between devices: 15.2 us -> 17 us  [swap(): return lax.ppermute(value, 'core', SWAP)]
    dot_general x12, matrix products: 4.31 us -> 2.61 us  [dot(): lax.dot_general(left, right, (((left_dim,), (right_dim,)), ((), ())), pre...]
    ppermute x12 -> x15, waiting for transfers between devices: 10.1 us -> 8.81 us  [shift(): lax.ppermute(value, axis, [(i, (i + by) % count) for i in range(count)])]
  transfers between devices with their start and end apart: 20 -> 23, of which waited for: 10 -> 10; matrix products, arithmetic and copies ran while one was open for 7% -> 7% of each run, Pallas kernels for 0% -> 0%
where the time goes in v5:
time: 112 us; the launch traced here: 111 us
  starting transfers between devices  55.8 us (50%)
  waiting for transfers between devices  36.3 us (32%)
  Pallas kernels  7.98 us (7%)
  other arithmetic  3.4 us (3%)
  matrix products  3.28 us (3%)
  between operations  2.23 us (2%)
  local copies, waits for them, and re-layouts  2.19 us (2%)
    all_to_all x3, waiting for transfers between devices, exchange(): return lax.all_to_all(value, axes, 0, 0, tiled=True)  26.2 us
    ppermute x15, starting transfers between devices, shift(): lax.ppermute(value, axis, [(i, (i + by) % count) for i in range(count)])  22.4 us
    ppermute x5, starting transfers between devices, swap(): return lax.ppermute(value, 'core', SWAP)  17 us
    all_to_all x3, starting transfers between devices, exchange(): return lax.all_to_all(value, axes, 0, 0, tiled=True)  16.4 us
    ppermute x15, waiting for transfers between devices, shift(): lax.ppermute(value, axis, [(i, (i + by) % count) for i in range(count)])  8.81 us
    pallas_call x1, Pallas kernels, gather_rows(): pl.pallas_call(functools.partial(gather_kernel, per_step=per_step), out_s...  6.8 us
    dot_general x12, matrix products, dot(): lax.dot_general(left, right, (((left_dim,), (right_dim,)), ((), ())), pre...  2.61 us
  transfers between devices with their start and end apart: 23, of which 10 were waited for; matrix products, arithmetic and copies ran while one was open for 7% of the time, Pallas kernels for 0%

profile of v5, /device:TPU:1, one launch (start us, length us, event | category | flops | bytes accessed | tf_op | source)
XLA Modules:
  0.0 111.2 jit_solution(1684551233389498966)
XLA Ops:
  0.7 6.8 %gather_rows.1 = bf16[8,32,1536]{2,1,0:T(8,128)(2,1)} custom-call(s32[8,32]{1,0:T(8,128)} %bitcast.58, s32[1,32]{1,0:T(1,128)} %owners.1, bf16[16,32768]{1,0:T(8,128)(2,1)} %feats.1, bf16[32,8,128,128]{3,2,1,0:T(8,128)(2,1)} %bitcast.53, bf16[16,512]{1,0:T(8,128)(2,1)} %own.1, bf16[16,512]{1,0:T(8,128)(2,1)} %near.1), custom_call_target="tpu_custom_call" | custom-call | flops 134217728 | bytes 9437184 | tf_op jit(solution)/shard_map/gather_rows/pallas_call | solution.py:99
  7.5 9.1 %all-to-all-start = ((bf16[8,32,1536]{2,1,0:T(8,128)(2,1)}), bf16[8,32,1536]{2,1,0:T(8,128)(2,1)S(1)}, u32[]{:S(2)}, u32[]{:S(2)}) async-start(bf16[8,32,1536]{2,1,0:T(8,128)(2,1)} %gather_rows.1), calls=%async_computation | async-start | bytes 1572864 | tf_op jit(solution)/shard_map/all_to_all | solution.py:28
  16.6 1.0 collective-permute-start.5
  17.7 0.2 compare_reduce_fusion
  18.0 0.7 convolution_convert_fusion.3
  18.7 0.6 fusion.46
  20.9 2.8 %collective-permute-start.13 = (f32[8,256]{1,0:T(8,128)S(1)}, f32[8,256]{1,0:T(8,128)S(1)}, u32[]{:S(2)}, u32[]{:S(2)}) collective-permute-start(f32[8,256]{1,0:T(8,128)S(1)} %pad.4), channel_id=1, source_target_pairs={{0,192},{64,0},{128,64},{192,128},{1,193},{65,1},{129,65},{193,129... | collective-permute-start | bytes 24584 | tf_op jit(solution)/shard_map/ppermute | solution.py:40
  23.8 16.4 %all-to-all-done = bf16[8,32,1536]{2,1,0:T(8,128)(2,1)S(1)} async-done(((bf16[8,32,1536]{2,1,0:T(8,128)(2,1)}), bf16[8,32,1536]{2,1,0:T(8,128)(2,1)S(1)}, u32[]{:S(2)}, u32[]{:S(2)}) %all-to-all-start) | async-done | bytes 786464 | tf_op jit(solution)/shard_map/all_to_all | solution.py:28
  40.3 0.6 collective-permute-start
  40.8 0.2 convolution_convert_fusion
  41.0 0.2 fusion.10
  41.2 0.4 fusion.5
  41.6 1.0 collective-permute-done.refs_10_
  42.6 0.3 fusion
  43.0 2.8 %collective-permute-start.3 = (bf16[256,256]{1,0:T(8,128)(2,1)S(1)}, bf16[256,256]{1,0:T(8,128)(2,1)S(1)}, u32[]{:S(2)}, u32[]{:S(2)}) collective-permute-start(bf16[256,256]{1,0:T(8,128)(2,1)S(1)} %get-tuple-element.12), channel_id=1, source_target_pairs={{0,192},{64,0},{128,64},{192,128},{1,193},{65,1},{129,65},{193,129... | collective-permute-start | bytes 393224 | tf_op jit(solution)/shard_map/ppermute | solution.py:40
  45.8 1.6 %collective-permute-start.1 = (bf16[256,256]{1,0:T(8,128)(2,1)S(1)}, bf16[256,256]{1,0:T(8,128)(2,1)S(1)}, u32[]{:S(2)}, u32[]{:S(2)}) collective-permute-start(bf16[256,256]{1,0:T(8,128)(2,1)S(1)} %get-tuple-element.11), channel_id=1, source_target_pairs={{0,128},{64,192},{128,0},{192,64},{1,129},{65,193},{129,1},{193,65... | collective-permute-start | bytes 393224 | tf_op jit(solution)/shard_map/ppermute | solution.py:40
  47.4 0.2 fusion.12
  47.6 0.7 collective-permute-done.3
  48.3 2.4 %collective-permute-start.12 = (f32[8,256]{1,0:T(8,128)S(1)}, f32[8,256]{1,0:T(8,128)S(1)}, u32[]{:S(2)}, u32[]{:S(2)}) collective-permute-start(f32[8,256]{1,0:T(8,128)S(1)} %pad.4), channel_id=1, source_target_pairs={{0,128},{64,192},{128,0},{192,64},{1,129},{65,193},{129,1},{193,65... | collective-permute-start | bytes 24584 | tf_op jit(solution)/shard_map/ppermute | solution.py:40
  50.7 3.9 %collective-permute-done.2 = bf16[256,256]{1,0:T(8,128)(2,1)S(1)} collective-permute-done((bf16[256,256]{1,0:T(8,128)(2,1)S(1)}, bf16[256,256]{1,0:T(8,128)(2,1)S(1)}, u32[]{:S(2)}, u32[]{:S(2)}) %collective-permute-start.2) | collective-permute-done | bytes 131104 | tf_op jit(solution)/shard_map/ppermute | solution.py:40
  55.0 0.2 convolution_convert_fusion.5
  55.3 0.2 convolution_convert_fusion.4
  55.6 0.3 fusion.2.refs_0_
  55.9 0.4 collective-permute-start.6
  56.3 3.6 %collective-permute-start.7 = (bf16[256,256]{1,0:T(8,128)(2,1)S(1)}, bf16[256,256]{1,0:T(8,128)(2,1)S(1)}, u32[]{:S(2)}, u32[]{:S(2)}) collective-permute-start(bf16[256,256]{1,0:T(8,128)(2,1)S(1)} %fusion.2.refs_0_), channel_id=1, source_target_pairs={{0,192},{64,0},{128,64},{192,128},{1,193},{65,1},{129,65},{193,129... | collective-permute-start | bytes 393224 | tf_op jit(solution)/shard_map/ppermute | solution.py:40
  59.8 1.3 %collective-permute-start.10 = (bf16[64,256]{1,0:T(8,128)(2,1)S(1)}, bf16[64,256]{1,0:T(8,128)(2,1)S(1)}, u32[]{:S(2)}, u32[]{:S(2)}) collective-permute-start(bf16[64,256]{1,0:T(8,128)(2,1)S(1)} %get-tuple-element.17), channel_id=1, source_target_pairs={{0,128},{64,192},{128,0},{192,64},{1,129},{65,193},{129,1},{193,65... | collective-permute-start | bytes 98312 | tf_op jit(solution)/shard_map/ppermute | solution.py:40
  61.1 2.0 %collective-permute-start.11 = (bf16[64,256]{1,0:T(8,128)(2,1)S(1)}, bf16[64,256]{1,0:T(8,128)(2,1)S(1)}, u32[]{:S(2)}, u32[]{:S(2)}) collective-permute-start(bf16[64,256]{1,0:T(8,128)(2,1)S(1)} %get-tuple-element.14), channel_id=1, source_target_pairs={{0,64},{64,128},{128,192},{192,0},{1,65},{65,129},{129,193},{193,1... | collective-permute-start | bytes 98312 | tf_op jit(solution)/shard_map/ppermute | solution.py:40
  63.1 2.4 %collective-permute-done.10.refs_6_ = bf16[64,256]{1,0:T(8,128)(2,1)S(1)} collective-permute-done((bf16[64,256]{1,0:T(8,128)(2,1)S(1)}, bf16[64,256]{1,0:T(8,128)(2,1)S(1)}, u32[]{:S(2)}, u32[]{:S(2)}) %collective-permute-start.10) | collective-permute-done | bytes 32800 | tf_op jit(solution)/shard_map/ppermute | solution.py:40
  65.5 0.6 collective-permute-done.11.refs_7_
  66.1 1.2 %grad_parts.1 = bf16[8,80,256]{2,1,0:T(8,128)(2,1)} custom-call(bf16[256,256]{1,0:T(8,128)(2,1)S(1)} %fusion.2.refs_0_, bf16[256,256]{1,0:T(8,128)(2,1)S(1)} %collective-permute-done.6.refs_1_, bf16[256,256]{1,0:T(8,128)(2,1)S(1)} %collective-permute-done.7.refs_2_, bf16[256,256]{1,0:T(8,128)(2,1)S(1)} %collective-permute-done.8.refs_3_, ...), custom_call_target="tpu_custom_call" | custom-call | flops 268435456 | bytes 1966080 | tf_op jit(solution)/shard_map/grad_parts/pallas_call | solution.py:147
  67.3 3.4 %all-to-all-start.1 = ((bf16[8,80,256]{2,1,0:T(8,128)(2,1)}), bf16[8,80,256]{2,1,0:T(8,128)(2,1)S(1)}, u32[]{:S(2)}, u32[]{:S(2)}) async-start(bf16[8,80,256]{2,1,0:T(8,128)(2,1)} %grad_parts.1), calls=%async_computation.1 | async-start | bytes 655360 | tf_op jit(solution)/shard_map/all_to_all | solution.py:28
  71.1 2.9 %collective-permute-start.4 = (f32[128,128]{1,0:T(8,128)S(1)}, f32[128,128]{1,0:T(8,128)S(1)}, u32[]{:S(2)}, u32[]{:S(2)}) collective-permute-start(f32[128,128]{1,0:T(8,128)S(1)} %slice_select_fusion), channel_id=1, source_target_pairs={{0,4},{4,0},{1,5},{5,1},{2,6},{6,2},{3,7},{7,3},{8,12},{12,8},{9,1... | collective-permute-start | bytes 196616 | tf_op jit(solution)/shard_map/ppermute | solution.py:36
  74.0 6.7 %all-to-all-done.1 = bf16[8,80,256]{2,1,0:T(8,128)(2,1)S(1)} async-done(((bf16[8,80,256]{2,1,0:T(8,128)(2,1)}), bf16[8,80,256]{2,1,0:T(8,128)(2,1)S(1)}, u32[]{:S(2)}, u32[]{:S(2)}) %all-to-all-start.1) | async-done | bytes 327712 | tf_op jit(solution)/shard_map/all_to_all | solution.py:28
  80.7 2.8 %collective-permute-start.17 = (f32[80,256]{1,0:T(8,128)S(1)}, f32[80,256]{1,0:T(8,128)S(1)}, u32[]{:S(2)}, u32[]{:S(2)}) collective-permute-start(f32[80,256]{1,0:T(8,128)S(1)} %convert_reduce_fusion), channel_id=1, source_target_pairs={{0,2},{1,3},{2,0},{3,1},{4,6},{5,7},{6,4},{7,5},{8,10},{9,11},{10,... | collective-permute-start | bytes 245768 | tf_op jit(solution)/shard_map/ppermute | solution.py:40
  83.6 0.3 collective-permute-start.15
  83.9 2.4 %collective-permute-start.16 = (f32[80,256]{1,0:T(8,128)S(1)}, f32[80,256]{1,0:T(8,128)S(1)}, u32[]{:S(2)}, u32[]{:S(2)}) collective-permute-start(f32[80,256]{1,0:T(8,128)S(1)} %convert_reduce_fusion), channel_id=1, source_target_pairs={{0,3},{1,0},{2,1},{3,2},{4,7},{5,4},{6,5},{7,6},{8,11},{9,8},{10,9... | collective-permute-start | bytes 245768 | tf_op jit(solution)/shard_map/ppermute | solution.py:40
  86.3 0.6 fusion.21
  86.9 1.2 %collective-permute-done.15 = f32[80,256]{1,0:T(8,128)S(1)} collective-permute-done((f32[80,256]{1,0:T(8,128)S(1)}, f32[80,256]{1,0:T(8,128)S(1)}, u32[]{:S(2)}, u32[]{:S(2)}) %collective-permute-start.15) | collective-permute-done | bytes 81952 | tf_op jit(solution)/shard_map/ppermute | solution.py:40
  88.1 0.7 broadcast_in_dim.8
  88.8 3.9 %all-to-all-start.2 = ((f32[32,8,256]{2,1,0:T(8,128)}), f32[32,8,256]{2,1,0:T(8,128)S(1)}, u32[]{:S(2)}, u32[]{:S(2)}) async-start(f32[32,8,256]{2,1,0:T(8,128)} %broadcast_in_dim.8), calls=%async_computation.2 | async-start | bytes 524288 | tf_op jit(solution)/shard_map/all_to_all | solution.py:28
  92.7 5.7 %collective-permute-start.18 = (f32[40,256]{1,0:T(8,128)S(1)}, f32[40,256]{1,0:T(8,128)S(1)}, u32[]{:S(2)}, u32[]{:S(2)}) collective-permute-start(f32[40,256]{1,0:T(8,128)S(1)} %pad_maximum_fusion.5), channel_id=1, source_target_pairs={{0,4},{4,0},{1,5},{5,1},{2,6},{6,2},{3,7},{7,3},{8,12},{12,8},{9,1... | collective-permute-start | bytes 122888 | tf_op jit(solution)/shard_map/ppermute | solution.py:36
  98.4 0.5 slice_bitcast_fusion
  99.0 0.4 collective-permute-done.18
  99.3 3.1 %all-to-all-done.2 = f32[32,8,256]{2,1,0:T(8,128)S(1)} async-done(((f32[32,8,256]{2,1,0:T(8,128)}), f32[32,8,256]{2,1,0:T(8,128)S(1)}, u32[]{:S(2)}, u32[]{:S(2)}) %all-to-all-start.2) | async-done | bytes 262176 | tf_op jit(solution)/shard_map/all_to_all | solution.py:28
  102.4 6.8 %collective-permute-start.19 = (f32[256,256]{1,0:T(8,128)S(1)}, f32[256,256]{1,0:T(8,128)S(1)}, u32[]{:S(2)}, u32[]{:S(2)}) collective-permute-start(f32[256,256]{1,0:T(8,128)S(1)} %bitcast.54), channel_id=1, source_target_pairs={{0,4},{4,0},{1,5},{5,1},{2,6},{6,2},{3,7},{7,3},{8,12},{12,8},{9,1... | collective-permute-start | bytes 786440 | tf_op jit(solution)/shard_map/ppermute | solution.py:36
  109.2 0.6 pad_maximum_fusion.7
  109.7 0.6 pad_maximum_fusion.6
  110.4 0.8 pad_maximum_fusion
  (59 shorter events, 1.7 us)
Async XLA Ops:
  0.6 17.3 %copy-start = (bf16[1,32,128,128]{3,2,1,0:T(8,128)(2,1)S(1)}, bf16[1,32,128,128]{3,2,1,0:T(8,128)(2,1)}, u32[]{:S(2)}) copy-start(bf16[1,32,128,128]{3,2,1,0:T(8,128)(2,1)} %param.15) | copy-start | bytes 3145732
  0.7 17.0 %copy-start.4 = (s32[1,32]{1,0:T(1,128)S(1)}, s32[1,32]{1,0:T(1,128)}, u32[]{:S(2)}) copy-start(s32[1,32]{1,0:T(1,128)} %owners.1) | copy-start | bytes 388
  0.7 16.0 %copy-start.3 = (bf16[1,128,128]{2,1,0:T(8,128)(2,1)S(1)}, bf16[1,128,128]{2,1,0:T(8,128)(2,1)}, u32[]{:S(2)}) copy-start(bf16[1,128,128]{2,1,0:T(8,128)(2,1)} %param.23) | copy-start | bytes 98308
  0.7 20.0 %copy-start.6 = (f32[512]{0:T(512)S(1)}, f32[512]{0:T(512)}, u32[]{:S(2)}) copy-start(f32[512]{0:T(512)} %param.19) | copy-start | bytes 6148
  0.7 40.2 %copy-start.1 = (bf16[512,128]{1,0:T(8,128)(2,1)S(1)}, bf16[512,128]{1,0:T(8,128)(2,1)}, u32[]{:S(2)}) copy-start(bf16[512,128]{1,0:T(8,128)(2,1)} %param.21) | copy-start | bytes 393220
  7.5 48.1 %copy-start.2 = (bf16[512,128]{1,0:T(8,128)(2,1)S(1)}, bf16[512,128]{1,0:T(8,128)(2,1)}, u32[]{:S(2)}) copy-start(bf16[512,128]{1,0:T(8,128)(2,1)} %param.20) | copy-start | bytes 393220
  7.5 32.7 %all-to-all-start = ((bf16[8,32,1536]{2,1,0:T(8,128)(2,1)}), bf16[8,32,1536]{2,1,0:T(8,128)(2,1)S(1)}, u32[]{:S(2)}, u32[]{:S(2)}) async-start(bf16[8,32,1536]{2,1,0:T(8,128)(2,1)} %gather_rows.1), calls=%async_computation | async-start | bytes 1572864 | tf_op jit(solution)/shard_map/all_to_all | solution.py:28
  16.6 4.1 %collective-permute-start.5 = (bf16[128,128]{1,0:T(8,128)(2,1)S(1)}, bf16[128,128]{1,0:T(8,128)(2,1)S(1)}, u32[]{:S(2)}, u32[]{:S(2)}) collective-permute-start(bf16[128,128]{1,0:T(8,128)(2,1)S(1)} %bitcast.55), channel_id=1, source_target_pairs={{0,4},{4,0},{1,5},{5,1},{2,6},{6,2},{3,7},{7,3},{8,12},{12,8},{9,1... | collective-permute-start | bytes 98312 | tf_op jit(solution)/shard_map/ppermute | solution.py:36
  18.6 67.6 %copy-start.5 = (f32[128]{0:T(128)S(1)}, f32[128]{0:T(128)}, u32[]{:S(2)}) copy-start(f32[128]{0:T(128)} %param.22) | copy-start | bytes 1540
  20.9 35.4 %collective-permute-start.13 = (f32[8,256]{1,0:T(8,128)S(1)}, f32[8,256]{1,0:T(8,128)S(1)}, u32[]{:S(2)}, u32[]{:S(2)}) collective-permute-start(f32[8,256]{1,0:T(8,128)S(1)} %pad.4), channel_id=1, source_target_pairs={{0,192},{64,0},{128,64},{192,128},{1,193},{65,1},{129,65},{193,129... | collective-permute-start | bytes 24584 | tf_op jit(solution)/shard_map/ppermute | solution.py:40
  23.7 36.1 %collective-permute-start.14 = (f32[8,256]{1,0:T(8,128)S(1)}, f32[8,256]{1,0:T(8,128)S(1)}, u32[]{:S(2)}, u32[]{:S(2)}) collective-permute-start(f32[8,256]{1,0:T(8,128)S(1)} %pad.4), channel_id=1, source_target_pairs={{0,64},{64,128},{128,192},{192,0},{1,65},{65,129},{129,193},{193,1... | collective-permute-start | bytes 24584 | tf_op jit(solution)/shard_map/ppermute | solution.py:40
  40.3 2.3 %collective-permute-start = (bf16[256,1280]{1,0:T(8,128)(2,1)S(1)}, bf16[256,1280]{1,0:T(8,128)(2,1)S(1)}, u32[]{:S(2)}, u32[]{:S(2)}) collective-permute-start(bf16[256,1280]{1,0:T(8,128)(2,1)S(1)} %slice.138), channel_id=1, source_target_pairs={{0,4},{4,0},{1,5},{5,1},{2,6},{6,2},{3,7},{7,3},{8,12},{12,8},{9,1... | collective-permute-start | bytes 1966088 | tf_op jit(solution)/shard_map/ppermute | solution.py:36
  43.0 5.3 %collective-permute-start.3 = (bf16[256,256]{1,0:T(8,128)(2,1)S(1)}, bf16[256,256]{1,0:T(8,128)(2,1)S(1)}, u32[]{:S(2)}, u32[]{:S(2)}) collective-permute-start(bf16[256,256]{1,0:T(8,128)(2,1)S(1)} %get-tuple-element.12), channel_id=1, source_target_pairs={{0,192},{64,0},{128,64},{192,128},{1,193},{65,1},{129,65},{193,129... | collective-permute-start | bytes 393224 | tf_op jit(solution)/shard_map/ppermute | solution.py:40
  45.8 8.8 %collective-permute-start.2 = (bf16[256,256]{1,0:T(8,128)(2,1)S(1)}, bf16[256,256]{1,0:T(8,128)(2,1)S(1)}, u32[]{:S(2)}, u32[]{:S(2)}) collective-permute-start(bf16[256,256]{1,0:T(8,128)(2,1)S(1)} %get-tuple-element.13), channel_id=1, source_target_pairs={{0,64},{64,128},{128,192},{192,0},{1,65},{65,129},{129,193},{193,1... | collective-permute-start | bytes 393224 | tf_op jit(solution)/shard_map/ppermute | solution.py:40
  45.8 8.8 %collective-permute-start.1 = (bf16[256,256]{1,0:T(8,128)(2,1)S(1)}, bf16[256,256]{1,0:T(8,128)(2,1)S(1)}, u32[]{:S(2)}, u32[]{:S(2)}) collective-permute-start(bf16[256,256]{1,0:T(8,128)(2,1)S(1)} %get-tuple-element.11), channel_id=1, source_target_pairs={{0,128},{64,192},{128,0},{192,64},{1,129},{65,193},{129,1},{193,65... | collective-permute-start | bytes 393224 | tf_op jit(solution)/shard_map/ppermute | solution.py:40
  48.3 11.5 %collective-permute-start.12 = (f32[8,256]{1,0:T(8,128)S(1)}, f32[8,256]{1,0:T(8,128)S(1)}, u32[]{:S(2)}, u32[]{:S(2)}) collective-permute-start(f32[8,256]{1,0:T(8,128)S(1)} %pad.4), channel_id=1, source_target_pairs={{0,128},{64,192},{128,0},{192,64},{1,129},{65,193},{129,1},{193,65... | collective-permute-start | bytes 24584 | tf_op jit(solution)/shard_map/ppermute | solution.py:40
  55.5 5.6 %collective-permute-start.9 = (bf16[64,256]{1,0:T(8,128)(2,1)S(1)}, bf16[64,256]{1,0:T(8,128)(2,1)S(1)}, u32[]{:S(2)}, u32[]{:S(2)}) collective-permute-start(bf16[64,256]{1,0:T(8,128)(2,1)S(1)} %get-tuple-element.16), channel_id=1, source_target_pairs={{0,192},{64,0},{128,64},{192,128},{1,193},{65,1},{129,65},{193,129... | collective-permute-start | bytes 98312 | tf_op jit(solution)/shard_map/ppermute | solution.py:40
  55.9 10.2 %collective-permute-start.6 = (bf16[256,256]{1,0:T(8,128)(2,1)S(1)}, bf16[256,256]{1,0:T(8,128)(2,1)S(1)}, u32[]{:S(2)}, u32[]{:S(2)}) collective-permute-start(bf16[256,256]{1,0:T(8,128)(2,1)S(1)} %fusion.2.refs_0_), channel_id=1, source_target_pairs={{0,128},{64,192},{128,0},{192,64},{1,129},{65,193},{129,1},{193,65... | collective-permute-start | bytes 393224 | tf_op jit(solution)/shard_map/ppermute | solution.py:40
  56.3 9.8 %collective-permute-start.7 = (bf16[256,256]{1,0:T(8,128)(2,1)S(1)}, bf16[256,256]{1,0:T(8,128)(2,1)S(1)}, u32[]{:S(2)}, u32[]{:S(2)}) collective-permute-start(bf16[256,256]{1,0:T(8,128)(2,1)S(1)} %fusion.2.refs_0_), channel_id=1, source_target_pairs={{0,192},{64,0},{128,64},{192,128},{1,193},{65,1},{129,65},{193,129... | collective-permute-start | bytes 393224 | tf_op jit(solution)/shard_map/ppermute | solution.py:40
  59.8 6.3 %collective-permute-start.8 = (bf16[256,256]{1,0:T(8,128)(2,1)S(1)}, bf16[256,256]{1,0:T(8,128)(2,1)S(1)}, u32[]{:S(2)}, u32[]{:S(2)}) collective-permute-start(bf16[256,256]{1,0:T(8,128)(2,1)S(1)} %fusion.2.refs_0_), channel_id=1, source_target_pairs={{0,64},{64,128},{128,192},{192,0},{1,65},{65,129},{129,193},{193,1... | collective-permute-start | bytes 393224 | tf_op jit(solution)/shard_map/ppermute | solution.py:40
  59.8 5.7 %collective-permute-start.10 = (bf16[64,256]{1,0:T(8,128)(2,1)S(1)}, bf16[64,256]{1,0:T(8,128)(2,1)S(1)}, u32[]{:S(2)}, u32[]{:S(2)}) collective-permute-start(bf16[64,256]{1,0:T(8,128)(2,1)S(1)} %get-tuple-element.17), channel_id=1, source_target_pairs={{0,128},{64,192},{128,0},{192,64},{1,129},{65,193},{129,1},{193,65... | collective-permute-start | bytes 98312 | tf_op jit(solution)/shard_map/ppermute | solution.py:40
  61.1 5.0 %collective-permute-start.11 = (bf16[64,256]{1,0:T(8,128)(2,1)S(1)}, bf16[64,256]{1,0:T(8,128)(2,1)S(1)}, u32[]{:S(2)}, u32[]{:S(2)}) collective-permute-start(bf16[64,256]{1,0:T(8,128)(2,1)S(1)} %get-tuple-element.14), channel_id=1, source_target_pairs={{0,64},{64,128},{128,192},{192,0},{1,65},{65,129},{129,193},{193,1... | collective-permute-start | bytes 98312 | tf_op jit(solution)/shard_map/ppermute | solution.py:40
  67.3 13.4 %all-to-all-start.1 = ((bf16[8,80,256]{2,1,0:T(8,128)(2,1)}), bf16[8,80,256]{2,1,0:T(8,128)(2,1)S(1)}, u32[]{:S(2)}, u32[]{:S(2)}) async-start(bf16[8,80,256]{2,1,0:T(8,128)(2,1)} %grad_parts.1), calls=%async_computation.1 | async-start | bytes 655360 | tf_op jit(solution)/shard_map/all_to_all | solution.py:28
  71.1 15.1 %collective-permute-start.4 = (f32[128,128]{1,0:T(8,128)S(1)}, f32[128,128]{1,0:T(8,128)S(1)}, u32[]{:S(2)}, u32[]{:S(2)}) collective-permute-start(f32[128,128]{1,0:T(8,128)S(1)} %slice_select_fusion), channel_id=1, source_target_pairs={{0,4},{4,0},{1,5},{5,1},{2,6},{6,2},{3,7},{7,3},{8,12},{12,8},{9,1... | collective-permute-start | bytes 196616 | tf_op jit(solution)/shard_map/ppermute | solution.py:36
  80.7 6.2 %collective-permute-start.17 = (f32[80,256]{1,0:T(8,128)S(1)}, f32[80,256]{1,0:T(8,128)S(1)}, u32[]{:S(2)}, u32[]{:S(2)}) collective-permute-start(f32[80,256]{1,0:T(8,128)S(1)} %convert_reduce_fusion), channel_id=1, source_target_pairs={{0,2},{1,3},{2,0},{3,1},{4,6},{5,7},{6,4},{7,5},{8,10},{9,11},{10,... | collective-permute-start | bytes 245768 | tf_op jit(solution)/shard_map/ppermute | solution.py:40
  83.6 4.5 %collective-permute-start.15 = (f32[80,256]{1,0:T(8,128)S(1)}, f32[80,256]{1,0:T(8,128)S(1)}, u32[]{:S(2)}, u32[]{:S(2)}) collective-permute-start(f32[80,256]{1,0:T(8,128)S(1)} %convert_reduce_fusion), channel_id=1, source_target_pairs={{0,1},{1,2},{2,3},{3,0},{4,5},{5,6},{6,7},{7,4},{8,9},{9,10},{10,1... | collective-permute-start | bytes 245768 | tf_op jit(solution)/shard_map/ppermute | solution.py:40
  83.9 4.2 %collective-permute-start.16 = (f32[80,256]{1,0:T(8,128)S(1)}, f32[80,256]{1,0:T(8,128)S(1)}, u32[]{:S(2)}, u32[]{:S(2)}) collective-permute-start(f32[80,256]{1,0:T(8,128)S(1)} %convert_reduce_fusion), channel_id=1, source_target_pairs={{0,3},{1,0},{2,1},{3,2},{4,7},{5,4},{6,5},{7,6},{8,11},{9,8},{10,9... | collective-permute-start | bytes 245768 | tf_op jit(solution)/shard_map/ppermute | solution.py:40
  88.8 13.5 %all-to-all-start.2 = ((f32[32,8,256]{2,1,0:T(8,128)}), f32[32,8,256]{2,1,0:T(8,128)S(1)}, u32[]{:S(2)}, u32[]{:S(2)}) async-start(f32[32,8,256]{2,1,0:T(8,128)} %broadcast_in_dim.8), calls=%async_computation.2 | async-start | bytes 524288 | tf_op jit(solution)/shard_map/all_to_all | solution.py:28
  92.7 6.6 %collective-permute-start.18 = (f32[40,256]{1,0:T(8,128)S(1)}, f32[40,256]{1,0:T(8,128)S(1)}, u32[]{:S(2)}, u32[]{:S(2)}) collective-permute-start(f32[40,256]{1,0:T(8,128)S(1)} %pad_maximum_fusion.5), channel_id=1, source_target_pairs={{0,4},{4,0},{1,5},{5,1},{2,6},{6,2},{3,7},{7,3},{8,12},{12,8},{9,1... | collective-permute-start | bytes 122888 | tf_op jit(solution)/shard_map/ppermute | solution.py:36
  102.4 8.0 %collective-permute-start.19 = (f32[256,256]{1,0:T(8,128)S(1)}, f32[256,256]{1,0:T(8,128)S(1)}, u32[]{:S(2)}, u32[]{:S(2)}) collective-permute-start(f32[256,256]{1,0:T(8,128)S(1)} %bitcast.54), channel_id=1, source_target_pairs={{0,4},{4,0},{1,5},{5,1},{2,6},{6,2},{3,7},{7,3},{8,12},{12,8},{9,1... | collective-permute-start | bytes 786440 | tf_op jit(solution)/shard_map/ppermute | solution.py:36
